TPU v7x, 512 devices: a whole 4x4x16 slice. The times are simulated.
512 devices in a mesh: seq: 64 (over x, z_lo, core), head: 8 (over y, z_hi).
Axes of the slice: x: 4, y: 4, z: 16 (z_hi: 2, z_lo: 8; z = z_hi * 8 + z_lo), core: 2. Of those that a mesh axis runs over, the one named last changes fastest.
Arguments:
- queries: bfloat16 [16384, 8192], P(('seq', 'head')), may hold values from -8 to 8
- cache_keys: bfloat16 [4096, 1024], P('seq', 'head'), may hold values from -4 to 4
- cache_values: bfloat16 [4096, 1024], P('seq', 'head'), may hold values from -4 to 4
- slab_keys: bfloat16 [16384, 1024], P('seq', 'head'), may hold values from -4 to 4
- slab_values: bfloat16 [16384, 1024], P('seq', 'head'), may hold values from -4 to 4
- block_lists: int32 [64, 256, 24], P('head', 'seq'), may hold values from 0 to 63, as said below
Outputs:
- attended: bfloat16 [16384, 8192], P(('seq', 'head'))
Inputs may be any that keep to these rules, and one draw needn't show every extreme that they name: `block_lists`: for each head and query block the 24 entries are distinct. Entries 0 to 11 are the head's vertical blocks, the same for all its query blocks, all below 32, the first one 0. Entry 12 + j of query block q is 32 + (o_j + q) mod (32) for the head's own distinct offsets o_j.
All inputs are finite; a program needn't handle non-finite values.
Results may differ from a plain program's by a relative error of at most 0.0049.
Values may be sent and summed in bfloat16 or wider, within the bound.
No kernel may reach another device: no remote copies, remote signals or barrier semaphores. Data moves between devices by JAX's collectives and lax.ppermute only.
A program may use at most 64 MiB of HBM per device.

v0:
```python
import jax
import jax.numpy as jnp
from jax import lax
from jax.sharding import PartitionSpec as P

DH = 128
BLOCK = 64
WIN = 4


def softmax_weights(logit_matrix, allowed):
    masked = jnp.where(allowed, logit_matrix, -jnp.inf)
    highest = jnp.max(masked, axis=-1, keepdims=True)
    raised = jnp.exp(masked - highest)
    return (raised / jnp.sum(raised, axis=-1, keepdims=True)).astype(jnp.bfloat16)


def per_device(queries, cache_keys, cache_values, slab_keys, slab_values, block_lists):
    head_count = block_lists.shape[0]
    blocks_here = block_lists.shape[1]
    listed = block_lists.shape[2]
    kv_count = cache_keys.shape[1] // DH
    group_size = head_count // kv_count
    seq_position = lax.axis_index("seq")
    offsets = jnp.arange(WIN, dtype=jnp.int32)
    query_blocks = seq_position * blocks_here + jnp.arange(blocks_here, dtype=jnp.int32)
    slab_valid = query_blocks[:, None] - offsets[None, :] >= 0
    arrived = lax.all_to_all(queries, "head", split_axis=1, concat_axis=0, tiled=True)
    gathered_keys = lax.all_gather(cache_keys, "seq", axis=0, tiled=True)
    gathered_values = lax.all_gather(cache_values, "seq", axis=0, tiled=True)
    source_keys = lax.all_gather(slab_keys, "seq", axis=0, tiled=True)
    source_values = lax.all_gather(slab_values, "seq", axis=0, tiled=True)
    fetch_slab_index = jnp.maximum(query_blocks[:, None] - offsets[None, :], 0)
    fetched = (gathered_keys, gathered_values, source_keys, source_values, fetch_slab_index)
    gathered_keys, gathered_values, source_keys, source_values, slab_index = fetched

    def as_blocks(array):
        return array.reshape(array.shape[0] // BLOCK, BLOCK, kv_count, DH).transpose(2, 0, 1, 3)

    cache_key_blocks = as_blocks(gathered_keys)
    cache_value_blocks = as_blocks(gathered_values)
    slab_key_blocks = as_blocks(source_keys)
    slab_value_blocks = as_blocks(source_values)
    rows_in_block = jnp.arange(BLOCK, dtype=jnp.int32)
    causal = rows_in_block[None, :] <= rows_in_block[:, None]
    slab_mask = slab_valid[:, None, :, None] & (
        (offsets[None, None, :, None] > 0) | causal[None, :, None, :]
    )
    slab_mask = slab_mask.reshape(blocks_here, BLOCK, WIN * BLOCK)
    full_mask = jnp.concatenate(
        [jnp.ones((blocks_here, BLOCK, listed * BLOCK), dtype=bool), slab_mask], axis=2
    )
    query_heads = arrived.reshape(blocks_here, BLOCK, head_count, DH).transpose(2, 0, 1, 3)
    score_scale = DH ** (-0.5)

    def attend(query_tile_rows, lists, head_number):
        kv_number = head_number // group_size
        cache_k = lax.dynamic_index_in_dim(cache_key_blocks, kv_number, 0, keepdims=False)
        cache_v = lax.dynamic_index_in_dim(cache_value_blocks, kv_number, 0, keepdims=False)
        slab_k = lax.dynamic_index_in_dim(slab_key_blocks, kv_number, 0, keepdims=False)
        slab_v = lax.dynamic_index_in_dim(slab_value_blocks, kv_number, 0, keepdims=False)
        selected_key_rows = jnp.concatenate(
            [
                jnp.take(cache_k, lists, axis=0).reshape(blocks_here, listed * BLOCK, DH),
                jnp.take(slab_k, slab_index, axis=0).reshape(blocks_here, WIN * BLOCK, DH),
            ],
            axis=1,
        )
        selected_value_rows = jnp.concatenate(
            [
                jnp.take(cache_v, lists, axis=0).reshape(blocks_here, listed * BLOCK, DH),
                jnp.take(slab_v, slab_index, axis=0).reshape(blocks_here, WIN * BLOCK, DH),
            ],
            axis=1,
        )
        logit_matrix = (
            jnp.einsum(
                "yav,ycv->yac",
                query_tile_rows,
                selected_key_rows,
                preferred_element_type=jnp.float32,
            )
            * score_scale
        )
        probability_weights = softmax_weights(logit_matrix, full_mask)
        weighted_total = jnp.einsum(
            "fgx,fxc->fgc",
            probability_weights,
            selected_value_rows,
            preferred_element_type=jnp.float32,
        )
        return weighted_total.astype(jnp.bfloat16)

    pair_count = head_count // 2

    def attend_pair(item):
        pair_queries, pair_lists, pair_numbers = item
        return jax.vmap(attend)(pair_queries, pair_lists, pair_numbers)

    results = lax.map(
        attend_pair,
        (
            query_heads.reshape(pair_count, 2, blocks_here, BLOCK, DH),
            block_lists.reshape(pair_count, 2, blocks_here, listed),
            jnp.arange(head_count, dtype=jnp.int32).reshape(pair_count, 2),
        ),
    )
    results = results.reshape(head_count, blocks_here, BLOCK, DH).transpose(1, 2, 0, 3)
    results = results.reshape(blocks_here * BLOCK, head_count * DH)
    return lax.all_to_all(results, "head", split_axis=0, concat_axis=1, tiled=True)


def solution(mesh):
    return jax.shard_map(
        per_device,
        mesh=mesh,
        in_specs=(
            P(("seq", "head"), None),
            P("seq", "head"),
            P("seq", "head"),
            P("seq", "head"),
            P("seq", "head"),
            P("head", "seq", None),
        ),
        out_specs=P(("seq", "head"), None),
        check_vma=False,
    )
```

profile of v0, /device:TPU:32, one launch (start us, length us, event | category | flops | bytes accessed | tf_op | source)
XLA Modules:
  0.0 750.2 jit_solution(7762240975053461179)
XLA Ops:
  11.2 16.8 %all-to-all-start = ((bf16[32,8,1024]{2,0,1:T(8,128)(2,1)}), bf16[32,8,1024]{2,0,1:T(8,128)(2,1)S(1)}, u32[]{:S(2)}, u32[]{:S(2)}) async-start(bf16[32,8,1024]{2,0,1:T(8,128)(2,1)} %bitcast.61), calls=%async_computation | async-start | bytes 1048576 | tf_op jit(solution)/shard_map/all_to_all | solution.py:28
  29.6 35.1 %all-to-all-done = bf16[32,8,1024]{2,0,1:T(8,128)(2,1)S(1)} async-done(((bf16[32,8,1024]{2,0,1:T(8,128)(2,1)}), bf16[32,8,1024]{2,0,1:T(8,128)(2,1)S(1)}, u32[]{:S(2)}, u32[]{:S(2)}) %all-to-all-start) | async-done | bytes 524320 | tf_op jit(solution)/shard_map/all_to_all | solution.py:28
  65.6 79.8 %all-gather.5.cloned.1.call-done = bf16[4096,128]{1,0:T(8,128)(2,1)} async-done(((bf16[64,128]{1,0:T(8,128)(2,1)}), bf16[4096,128]{1,0:T(8,128)(2,1)}) %all-gather.5.cloned.1.call-update) | async-done | bytes 1048592 | tf_op jit(solution)/shard_map/all_gather | solution.py:29
  145.4 119.9 %all-gather.9.cloned.1.call-done = bf16[4096,128]{1,0:T(8,128)(2,1)} async-done(((bf16[64,128]{1,0:T(8,128)(2,1)}), bf16[4096,128]{1,0:T(8,128)(2,1)}) %all-gather.9.cloned.1.call-update) | async-done | bytes 1048592 | tf_op jit(solution)/shard_map/all_gather | solution.py:30
  265.3 121.0 %all-gather.7.cloned.1.call-done = bf16[16384,128]{1,0:T(8,128)(2,1)} async-done(((bf16[256,128]{1,0:T(8,128)(2,1)}), bf16[16384,128]{1,0:T(8,128)(2,1)}) %all-gather.7.cloned.1.call-update) | async-done | bytes 4194320 | tf_op jit(solution)/shard_map/all_gather | solution.py:31
  386.3 120.4 %all-gather.11.cloned.1.call-done = bf16[16384,128]{1,0:T(8,128)(2,1)} async-done(((bf16[256,128]{1,0:T(8,128)(2,1)}), bf16[16384,128]{1,0:T(8,128)(2,1)}) %all-gather.11.cloned.1.call-update) | async-done | bytes 4194320 | tf_op jit(solution)/shard_map/all_gather | solution.py:32
  506.7 188.8 %while.14 = (s32[]{:T(128)}, bf16[4,2,4,64,128]{4,3,2,1,0:T(8,128)(2,1)}, pred[4,64,1792]{2,1,0:T(8,128)(4,1)}, bf16[4,2,4,64,128]{4,1,0,3,2:T(2,128)(2,1)}, bf1...) while((s32[]{:T(128)}, ...), condition=%wide.region_3.6_spmd.clone.clone, body=%wide.region_0.5_spmd.clone.clone.sunk | while | flops 494608064 | bytes 110837584 | solution.py:100
  506.7 7.8 %broadcast.365 = bf16[2,256,64,128]{3,2,1,0:T(8,128)(2,1)} broadcast(bf16[256,64,128]{2,1,0:T(8,128)(2,1)} %bitcast.104), dimensions={1,2,3} | broadcast | bytes 12582912 | tf_op jit(solution)/shard_map/while/body/eval_jaxpr/vmap(jit(dynamic_index_in_dim))/squeeze | solution.py:60
  518.8 7.8 %broadcast.366 = bf16[2,256,64,128]{3,2,1,0:T(8,128)(2,1)} broadcast(bf16[256,64,128]{2,1,0:T(8,128)(2,1)} %bitcast.106), dimensions={1,2,3} | broadcast | bytes 12582912 | tf_op jit(solution)/shard_map/while/body/eval_jaxpr/vmap(jit(dynamic_index_in_dim))/squeeze | solution.py:61
  526.6 4.1 gather_fusion.1
  548.9 5.0 fusion.38
  553.9 7.8 %broadcast.365 = bf16[2,256,64,128]{3,2,1,0:T(8,128)(2,1)} broadcast(bf16[256,64,128]{2,1,0:T(8,128)(2,1)} %bitcast.104), dimensions={1,2,3} | broadcast | bytes 12582912 | tf_op jit(solution)/shard_map/while/body/eval_jaxpr/vmap(jit(dynamic_index_in_dim))/squeeze | solution.py:60
  566.0 7.8 %broadcast.366 = bf16[2,256,64,128]{3,2,1,0:T(8,128)(2,1)} broadcast(bf16[256,64,128]{2,1,0:T(8,128)(2,1)} %bitcast.106), dimensions={1,2,3} | broadcast | bytes 12582912 | tf_op jit(solution)/shard_map/while/body/eval_jaxpr/vmap(jit(dynamic_index_in_dim))/squeeze | solution.py:61
  573.8 4.1 gather_fusion.1
  596.1 5.0 fusion.38
  601.1 7.8 %broadcast.365 = bf16[2,256,64,128]{3,2,1,0:T(8,128)(2,1)} broadcast(bf16[256,64,128]{2,1,0:T(8,128)(2,1)} %bitcast.104), dimensions={1,2,3} | broadcast | bytes 12582912 | tf_op jit(solution)/shard_map/while/body/eval_jaxpr/vmap(jit(dynamic_index_in_dim))/squeeze | solution.py:60
  613.1 7.8 %broadcast.366 = bf16[2,256,64,128]{3,2,1,0:T(8,128)(2,1)} broadcast(bf16[256,64,128]{2,1,0:T(8,128)(2,1)} %bitcast.106), dimensions={1,2,3} | broadcast | bytes 12582912 | tf_op jit(solution)/shard_map/while/body/eval_jaxpr/vmap(jit(dynamic_index_in_dim))/squeeze | solution.py:61
  621.0 4.1 gather_fusion.1
  643.3 5.0 fusion.38
  648.2 7.8 %broadcast.365 = bf16[2,256,64,128]{3,2,1,0:T(8,128)(2,1)} broadcast(bf16[256,64,128]{2,1,0:T(8,128)(2,1)} %bitcast.104), dimensions={1,2,3} | broadcast | bytes 12582912 | tf_op jit(solution)/shard_map/while/body/eval_jaxpr/vmap(jit(dynamic_index_in_dim))/squeeze | solution.py:60
  660.3 7.8 %broadcast.366 = bf16[2,256,64,128]{3,2,1,0:T(8,128)(2,1)} broadcast(bf16[256,64,128]{2,1,0:T(8,128)(2,1)} %bitcast.106), dimensions={1,2,3} | broadcast | bytes 12582912 | tf_op jit(solution)/shard_map/while/body/eval_jaxpr/vmap(jit(dynamic_index_in_dim))/squeeze | solution.py:61
  668.1 4.1 gather_fusion.1
  690.4 5.0 fusion.38
  697.0 45.8 %all_to_all.35 = bf16[8,32,1024]{2,1,0:T(8,128)(2,1)S(1)} all-to-all(bf16[8,32,1024]{2,1,0:T(8,128)(2,1)S(1)} %all_to_all.29), channel_id=1, replica_groups=mesh['seq'=64,'head'=8] {'head'}, dimensions={0} | all-to-all | bytes 1048576 | tf_op jit(solution)/shard_map/all_to_all | solution.py:110
  (137 shorter events, 98.9 us)
Async XLA Ops:
  6.5 500.1 %copy-start.5 = (s32[8,4,24]{2,1,0:T(4,128)S(1)}, s32[8,4,24]{2,1,0:T(4,128)}, u32[]{:S(2)}) copy-start(s32[8,4,24]{2,1,0:T(4,128)} %param.17) | copy-start | bytes 9220
  6.5 138.8 %all-gather.5.cloned.1.call-start = ((), (), s32[]{:S(2)}) async-start(), calls=%async_computation.2 | async-start | bytes 1064960 | tf_op jit(solution)/shard_map/all_gather | solution.py:29
  7.3 258.0 %all-gather.9.cloned.1.call-start = ((), (), s32[]{:S(2)}) async-start(), calls=%async_computation.4 | async-start | bytes 1064960 | tf_op jit(solution)/shard_map/all_gather | solution.py:30
  8.0 378.3 %all-gather.7.cloned.1.call-start = ((), (), s32[]{:S(2)}) async-start(), calls=%async_computation.3 | async-start | bytes 4259840 | tf_op jit(solution)/shard_map/all_gather | solution.py:31
  8.7 497.9 %all-gather.11.cloned.1.call-start = ((), (), s32[]{:S(2)}) async-start(), calls=%async_computation.5 | async-start | bytes 4259840 | tf_op jit(solution)/shard_map/all_gather | solution.py:32
  11.2 53.5 %all-to-all-start = ((bf16[32,8,1024]{2,0,1:T(8,128)(2,1)}), bf16[32,8,1024]{2,0,1:T(8,128)(2,1)S(1)}, u32[]{:S(2)}, u32[]{:S(2)}) async-start(bf16[32,8,1024]{2,0,1:T(8,128)(2,1)} %bitcast.61), calls=%async_computation | async-start | bytes 1048576 | tf_op jit(solution)/shard_map/all_to_all | solution.py:28
  526.6 5.3 copy-start.1
  532.5 3.7 copy-start.2
  540.5 4.3 copy-start.3
  540.5 4.3 copy-start.4
  546.3 1.8 copy-start
  573.8 5.3 copy-start.1
  579.7 3.7 copy-start.2
  587.6 4.3 copy-start.3
  587.6 4.3 copy-start.4
  593.5 1.8 copy-start
  621.0 5.3 copy-start.1
  626.8 3.7 copy-start.2
  634.8 4.3 copy-start.3
  634.8 4.3 copy-start.4
  668.1 5.3 copy-start.1
  674.0 3.7 copy-start.2
  682.0 4.3 copy-start.3
  682.0 4.3 copy-start.4
  (2 other events, 3.6 us)
Sparse Core Ops, SparseCore 0:
  9.5 135.8 all-gather.4
  147.5 117.7 all-gather.8
  267.5 118.7 all-gather.6
  388.3 118.3 all-gather.10
where the time goes:
time: 751 us; the launch traced here: 750 us
  waiting for transfers between devices  479 us (64%)
  local copies, waits for them, and re-layouts  147 us (20%)
  blocking collectives  45.8 us (6%)
  matrix products  26.2 us (3%)
  other arithmetic  21.6 us (3%)
  starting transfers between devices  16.9 us (2%)
  between operations  13.2 us (2%)
    all_gather x1, waiting for transfers between devices, per_device(): source_keys = lax.all_gather(slab_keys, 'seq', axis=0, tiled=True)  121 us
    all_gather x1, waiting for transfers between devices, per_device(): source_values = lax.all_gather(slab_values, 'seq', axis=0, tiled=True)  120 us
    all_gather x1, waiting for transfers between devices, per_device(): gathered_values = lax.all_gather(cache_values, 'seq', axis=0, tiled=True)  120 us
    all_gather x1, waiting for transfers between devices, per_device(): gathered_keys = lax.all_gather(cache_keys, 'seq', axis=0, tiled=True)  79.8 us
    all_to_all x1, blocking collectives, per_device(): lax.all_to_all(results, 'head', split_axis=0, concat_axis=1, tiled=True)  45.8 us
    all_to_all x1, waiting for transfers between devices, per_device(): lax.all_to_all(queries, 'head', split_axis=1, concat_axis=0, tiled=True)  35.1 us
    squeeze x4, local copies, waits for them, and re-layouts, attend(): lax.dynamic_index_in_dim(slab_value_blocks, kv_number, 0, keepdims=False)  31.3 us
    squeeze x4, local copies, waits for them, and re-layouts, attend(): lax.dynamic_index_in_dim(slab_key_blocks, kv_number, 0, keepdims=False)  31.3 us
  transfers between devices with their start and end apart: 5, of which 5 were waited for; matrix products, arithmetic and copies ran while one was open for 1% of the time, Pallas kernels for 0%

commit v1 on v0

v1 whole, which is shorter than its diff:
```python
import functools
import math

import jax
import jax.numpy as jnp
from jax import lax
from jax.experimental import pallas as pl
from jax.experimental.pallas import tpu as pltpu
from jax.sharding import PartitionSpec as P

DH = 128
BLOCK = 64
NV = 12
WIN = 4
X, ZL, CORE = 4, 8, 2
CHUNKS = 2
NEG = -1e30
HEADS_A_STEP = 4


def attention_kernel(
    lists_ref, spot_ref, near_ref, far_ref, halo_ref, own_ref, *rest, pieces, blocks, listed
):
    piece_refs, (near_out, far_out, cache_ref, sem) = rest[:pieces], rest[pieces:]
    head = pl.program_id(0)
    rows = piece_refs[0].shape[0]
    half = BLOCK // 2

    @pl.when(head == 0)
    def _():
        copies = [
            pltpu.make_async_copy(ref, cache_ref.at[pl.ds(rows * i, rows)], sem.at[i])
            for i, ref in enumerate(piece_refs)
        ]
        for copy in copies:
            copy.start()
        for copy in copies:
            copy.wait()

    for lane in range(HEADS_A_STEP):
        base = (head * HEADS_A_STEP + lane) * (blocks * listed)
        lanes = slice(lane * DH, (lane + 1) * DH)
        factor = DH**-0.5 * math.log2(math.e)

        def rows_of(entry):
            return pl.ds(pl.multiple_of(lists_ref[entry] * BLOCK, BLOCK), BLOCK)

        def pick(entries, column):
            return jnp.concatenate(
                [cache_ref[rows_of(e), pl.ds(column, DH)] for e in entries], axis=0
            )

        def scores(a, b):
            return lax.dot_general(a, b, (((1,), (1,)), ((), ())), preferred_element_type=jnp.float32)

        def mix(a, b):
            return lax.dot_general(a, b, (((1,), (0,)), ((), ())), preferred_element_type=jnp.float32)

        def both(entries_0, entries_1, b, column):
            return jnp.concatenate(
                [
                    jnp.concatenate([pick(entries_0, column), window(b, column)], axis=0),
                    jnp.concatenate([pick(entries_1, column), window(b + 1, column)], axis=0),
                ],
                axis=1,
            )

        def window(b, column):
            parts = []
            if b < WIN - 1:
                parts.append(halo_ref[b * BLOCK : (WIN - 1) * BLOCK, column : column + DH])
            parts.append(own_ref[0 : (b + 1) * BLOCK, column : column + DH])
            return jnp.concatenate(parts, axis=0)

        vertical = [base + j for j in range(NV)]
        q = jnp.concatenate(
            [ref[half * b : half * (b + 1), lanes] for b in range(blocks) for ref in (near_ref, far_ref)], axis=0
        )
        s_vertical = scores(q, pick(vertical, 0))
        window_at = (listed - NV) * BLOCK
        column = lax.broadcasted_iota(jnp.int32, (2 * BLOCK, WIN * BLOCK), 1)
        row = lax.broadcasted_iota(jnp.int32, (2 * BLOCK, WIN * BLOCK), 0)
        second = row >= BLOCK
        row = row % BLOCK
        row = jnp.where(row < half, row + spot_ref[1] * half, row - spot_ref[1] * half)
        causal = column <= row + (WIN - 1) * BLOCK
        first = spot_ref[0] == 0
        blank = jnp.zeros((BLOCK, DH), jnp.bfloat16)

        weights, mixes, totals = [], [], []
        for b in range(0, blocks, 2):
            here = slice(b * BLOCK, (b + 2) * BLOCK)
            slash = [[base + c * listed + j for j in range(NV, listed)] for c in (b, b + 1)]
            q_pair = jnp.concatenate(
                [
                    jnp.concatenate([q[b * BLOCK : (b + 1) * BLOCK], blank], axis=1),
                    jnp.concatenate([blank, q[(b + 1) * BLOCK : (b + 2) * BLOCK]], axis=1),
                ],
                axis=0,
            )
            s_v = s_vertical[here]
            s_p = scores(q_pair, both(*slash, b, 0))
            s_s, s_w = s_p[:, :window_at], s_p[:, window_at:]
            lowest = jnp.where(second, WIN - 2 - b, WIN - 1 - b) * jnp.where(first, BLOCK, 0)
            s_w = jnp.where(causal & (column >= lowest), s_w, NEG)
            top = jnp.maximum(
                jnp.maximum(jnp.max(s_v, axis=1, keepdims=True), jnp.max(s_s, axis=1, keepdims=True)),
                jnp.max(s_w, axis=1, keepdims=True),
            )
            shift = top * factor
            p_v = jnp.exp2(s_v * factor - shift)
            p_s = jnp.exp2(s_s * factor - shift)
            p_w = jnp.exp2(s_w * factor - shift)
            totals.append(
                jnp.sum(p_v, axis=1, keepdims=True)
                + jnp.sum(p_s, axis=1, keepdims=True)
                + jnp.sum(p_w, axis=1, keepdims=True)
            )
            weights.append(p_v.astype(jnp.bfloat16))
            p_p = jnp.concatenate([p_s.astype(jnp.bfloat16), p_w.astype(jnp.bfloat16)], axis=1)
            mixed = mix(p_p, both(*slash, b, DH))
            mixes += [mixed[:BLOCK, :DH], mixed[BLOCK:, DH:]]
        mixed = mix(jnp.concatenate(weights, axis=0), pick(vertical, DH)) + jnp.concatenate(mixes, axis=0)
        mixed = (mixed / jnp.concatenate(totals, axis=0)).astype(jnp.bfloat16)
        for b in range(blocks):
            near_out[half * b : half * (b + 1), lanes] = mixed[BLOCK * b : BLOCK * b + half]
            far_out[half * b : half * (b + 1), lanes] = mixed[BLOCK * b + half : BLOCK * (b + 1)]


def attention(lists, spot, near, far, halo, own, pieces, start, heads):
    group, blocks, listed = lists.shape
    tokens = far.shape[0]
    whole = pl.BlockSpec(memory_space=pltpu.VMEM)
    part = jax.ShapeDtypeStruct((tokens, heads * DH), jnp.bfloat16)
    return pl.pallas_call(
        functools.partial(attention_kernel, pieces=len(pieces), blocks=blocks, listed=listed),
        grid_spec=pltpu.PrefetchScalarGridSpec(
            num_scalar_prefetch=2,
            grid=(heads // HEADS_A_STEP,),
            in_specs=[
                pl.BlockSpec((tokens, HEADS_A_STEP * DH), lambda h, _, spot: (0, (spot[1] * group + start) // HEADS_A_STEP + h)),
                pl.BlockSpec((tokens, HEADS_A_STEP * DH), lambda h, *_: (0, h)),
                whole,
                whole,
                *[pl.BlockSpec(memory_space=pl.ANY)] * len(pieces),
            ],
            out_specs=[pl.BlockSpec((tokens, HEADS_A_STEP * DH), lambda h, *_: (0, h))] * 2,
            scratch_shapes=[
                pltpu.VMEM((sum(p.shape[0] for p in pieces), 2 * DH), jnp.bfloat16),
                pltpu.SemaphoreType.DMA((len(pieces),)),
            ],
        ),
        out_shape=[part, part],
        compiler_params=pltpu.CompilerParams(vmem_limit_bytes=40 * 2**20),
        cost_estimate=pl.CostEstimate(
            flops=8 * tokens * heads * DH * BLOCK * (listed + WIN),
            bytes_accessed=4 * 2**20,
            transcendentals=2 * tokens * heads * BLOCK * (listed + WIN),
        ),
        name="attention",
    )(lists[start : start + heads].reshape(-1), spot, near, far, halo, own, *pieces)


def per_device(queries, cache_keys, cache_values, slab_keys, slab_values, block_lists):
    count = X * ZL * CORE
    group = block_lists.shape[0]
    seq, side = lax.axis_index(("x", "zc")), lax.axis_index("zh")
    heads = group // CHUNKS

    def send(array, target):
        return lax.ppermute(array, ("x", "zc"), [(i, target(i)) for i in range(count)])

    def over_side(array):
        return lax.ppermute(array, "zh", [(0, 1), (1, 0)])

    slab = jnp.concatenate([slab_keys, slab_values], axis=1)
    halo = lax.ppermute(
        slab[-(WIN - 1) * BLOCK :], ("x", "zc"), [(i, i + 1) for i in range(count - 1)]
    )

    held = jnp.concatenate([cache_keys, cache_values], axis=1)
    order = [0]
    for bit in (4, 2, 1):
        held = jnp.concatenate([held, send(held, lambda i: i ^ (bit * CORE))], axis=0)
        order += [p | bit for p in order]
        if bit == 4:
            queries, held = lax.optimization_barrier((queries, held))
            near = lax.all_to_all(queries, "y", split_axis=1, concat_axis=0, tiled=True)
    leaving = [
        lax.dynamic_slice_in_dim(
            near, ((1 - side) * group + chunk * heads) * DH, heads * DH, axis=1
        )
        for chunk in range(CHUNKS)
    ]
    leaving, held, halo = lax.optimization_barrier((leaving, held, halo))
    far = [over_side(part) for part in leaving]
    copies = jnp.broadcast_to(held[None], (X, *held.shape))
    along_x = lax.all_to_all(copies, "x", split_axis=0, concat_axis=0, tiled=True)
    along_x = along_x.reshape(-1, 2 * DH)
    far[0], along_x = lax.optimization_barrier((far[0], along_x))
    pieces = [along_x, send(along_x, lambda i: i ^ 1)]

    place = [order.index(p) for p in range(ZL)]
    block_x, block_z, block_core = block_lists // (ZL * CORE), block_lists // CORE % ZL, block_lists % CORE
    own_z, own_core = seq // CORE % ZL, seq % CORE
    z_bits = block_z ^ own_z
    z_place = sum(jnp.where((z_bits & bit) != 0, place[bit], 0) for bit in (4, 2, 1))
    lists = (block_core ^ own_core) * (X * ZL) + block_x * ZL + z_place

    spot = jnp.stack([seq, side])
    mine, back = [], []
    for chunk in range(CHUNKS):
        here, theirs = attention(lists, spot, near, far[chunk], halo, slab, pieces, chunk * heads, heads)
        mine.append(here)
        back.append(over_side(theirs))
    both = jnp.where(
        side == 0, jnp.concatenate(mine + back, axis=1), jnp.concatenate(back + mine, axis=1)
    )
    return lax.all_to_all(both, "y", split_axis=0, concat_axis=1, tiled=True)


def solution(mesh):
    fine = jax.sharding.Mesh(mesh.devices.reshape(X, ZL * CORE, -1, 2), ("x", "zc", "y", "zh"))
    seq, head = ("x", "zc"), ("y", "zh")
    rows, columns = P((*seq, *head), None), P(seq, head)
    return jax.shard_map(
        per_device,
        mesh=fine,
        in_specs=(rows, columns, columns, columns, columns, P(head, seq, None)),
        out_specs=rows,
        check_vma=False,
    )
```

time: 751 us -> 135 us (0.18)
  waiting for transfers between devices: 479 us -> 32.8 us
  local copies, waits for them, and re-layouts: 147 us -> 6.12 us
  starting transfers between devices: 16.9 us -> 65.1 us
  blocking collectives: 45.8 us -> 17.8 us
  matrix products: 26.2 us -> 0 us
  other arithmetic: 21.6 us -> 1.29 us
  between operations: 13.2 us -> 0.24 us
  Pallas kernels: 0 us -> 10.9 us
    all_gather x4 -> x0, waiting for transfers between devices: 441 us -> none  [the longest x1 121 us: per_device(): source_keys = lax.all_gather(slab_keys, 'seq', axis=0, tiled=True)]
    squeeze x16 -> x0, local copies, waits for them, and re-layouts: 67.1 us -> none  [the longest x4 31.3 us: attend(): lax.dynamic_index_in_dim(slab_value_blocks, kv_number, 0, keepdims=False)]
    gather x20 -> x0, local copies, waits for them, and re-layouts: 62 us -> none  [the longest x4 16.5 us: attend(): jnp.take(slab_v, slab_index, axis=0).reshape(blocks_here, WIN * BLOCK, DH)]
    ppermute x0 -> x9, starting transfers between devices: none -> 56.4 us  [the longest x4 35.9 us: over_side(): return lax.ppermute(array, 'zh', [(0, 1), (1, 0)])]
    all_to_all x1 -> x2, waiting for transfers between devices: 35.1 us -> 1.78 us  [the longest x1 1.78 us: per_device(): near = lax.all_to_all(queries, 'y', split_axis=1, concat_axis=0, tiled=True)]
    ppermute x0 -> x9, waiting for transfers between devices: none -> 31 us  [the longest x4 26.5 us: over_side(): return lax.ppermute(array, 'zh', [(0, 1), (1, 0)])]
    all_to_all x1, blocking collectives: 45.8 us -> 17.8 us  [per_device(): return lax.all_to_all(both, 'y', split_axis=0, concat_axis=1, tiled=True)]
    dot_general x8 -> x0, matrix products: 26.2 us -> none  [the longest x4 19.9 us: attend(): jnp.einsum('fgx,fxc->fgc', probability_weights, selected_value_rows, pref...]
  transfers between devices with their start and end apart: 5 -> 11, of which waited for: 5 -> 7; matrix products, arithmetic and copies ran while one was open for 1% -> 2% of each run, Pallas kernels for 0% -> 8%
where the time goes in v1:
time: 135 us; the launch traced here: 134 us
  starting transfers between devices  65.1 us (48%)
  waiting for transfers between devices  32.8 us (24%)
  blocking collectives  17.8 us (13%)
  Pallas kernels  10.9 us (8%)
  local copies, waits for them, and re-layouts  6.12 us (5%)
    ppermute x4, starting transfers between devices, over_side(): return lax.ppermute(array, 'zh', [(0, 1), (1, 0)])  35.9 us
    ppermute x4, waiting for transfers between devices, over_side(): return lax.ppermute(array, 'zh', [(0, 1), (1, 0)])  26.5 us
    ppermute x4, starting transfers between devices, send(): lax.ppermute(array, ('x', 'zc'), [(i, target(i)) for i in range(count)])  18.5 us
    all_to_all x1, blocking collectives, per_device(): return lax.all_to_all(both, 'y', split_axis=0, concat_axis=1, tiled=True)  17.8 us
    pallas_call x2, Pallas kernels, attention(): pl.pallas_call(functools.partial(attention_kernel, pieces=len(pieces), bl...  10.9 us
    ppermute x4, waiting for transfers between devices, send(): lax.ppermute(array, ('x', 'zc'), [(i, target(i)) for i in range(count)])  4.51 us
    all_to_all x1, starting transfers between devices, per_device(): near = lax.all_to_all(queries, 'y', split_axis=1, concat_axis=0, tiled=True)  4.44 us
    all_to_all x1, starting transfers between devices, per_device(): lax.all_to_all(copies, 'x', split_axis=0, concat_axis=0, tiled=True)  4.29 us
  transfers between devices with their start and end apart: 11, of which 7 were waited for; matrix products, arithmetic and copies ran while one was open for 2% of the time, Pallas kernels for 8%

profile of v1, /device:TPU:32, one launch (start us, length us, event | category | flops | bytes accessed | tf_op | source)
XLA Modules:
  0.0 134.3 jit_solution(13820652487852178571)
XLA Ops:
  0.7 9.1 %collective-permute-start = (bf16[64,256]{1,0:T(8,128)(2,1)S(1)}, bf16[64,256]{1,0:T(8,128)(2,1)S(1)}, u32[]{:S(2)}, u32[]{:S(2)}) collective-permute-start(bf16[64,256]{1,0:T(8,128)(2,1)S(1)} %constant_dynamic-update-slice_fusion), channel_id=1, source_target_pairs={{0,64},{8,72},{16,80},{24,88},{32,96},{40,104},{48,112},{56,120},{... | collective-permute-start | bytes 98312 | tf_op jit(solution)/shard_map/ppermute | solution.py:171
  9.9 1.9 %collective-permute-done = bf16[64,256]{1,0:T(8,128)(2,1)S(1)} collective-permute-done((bf16[64,256]{1,0:T(8,128)(2,1)S(1)}, bf16[64,256]{1,0:T(8,128)(2,1)S(1)}, u32[]{:S(2)}, u32[]{:S(2)}) %collective-permute-start) | collective-permute-done | bytes 32800 | tf_op jit(solution)/shard_map/ppermute | solution.py:171
  11.7 5.2 %collective-permute-start.1 = (bf16[128,256]{1,0:T(8,128)(2,1)S(1)}, bf16[128,256]{1,0:T(8,128)(2,1)S(1)}, u32[]{:S(2)}, u32[]{:S(2)}) collective-permute-start(bf16[128,256]{1,0:T(8,128)(2,1)S(1)} %pad_maximum_fusion.2), channel_id=1, source_target_pairs={{0,32},{8,40},{16,48},{24,56},{32,0},{40,8},{48,16},{56,24},{64,96... | collective-permute-start | bytes 196616 | tf_op jit(solution)/shard_map/ppermute | solution.py:171
  16.9 1.9 %copy.12 = bf16[4,4,8,2048]{3,2,0,1:T(8,128)(2,1)} copy(bf16[4,4,8,2048]{3,2,1,0:T(8,128)(2,1)} %bitcast.26) | data formatting | bytes 1048576 | tf_op jit(solution)/shard_map/all_to_all | solution.py:188
  18.8 4.4 %all-to-all-start = ((bf16[32,4,2048]{2,0,1:T(8,128)(2,1)}), bf16[32,4,2048]{2,0,1:T(8,128)(2,1)S(1)}, u32[]{:S(2)}, u32[]{:S(2)}) async-start(bf16[32,4,2048]{2,0,1:T(8,128)(2,1)} %bitcast.16), calls=%async_computation | async-start | bytes 1048576 | tf_op jit(solution)/shard_map/all_to_all | solution.py:188
  23.3 2.3 %collective-permute-start.2 = (bf16[256,256]{1,0:T(8,128)(2,1)S(1)}, bf16[256,256]{1,0:T(8,128)(2,1)S(1)}, u32[]{:S(2)}, u32[]{:S(2)}) collective-permute-start(bf16[256,256]{1,0:T(8,128)(2,1)S(1)} %pad_maximum_fusion.1), channel_id=1, source_target_pairs={{0,16},{8,24},{16,0},{24,8},{32,48},{40,56},{48,32},{56,40},{64,80... | collective-permute-start | bytes 393224 | tf_op jit(solution)/shard_map/ppermute | solution.py:171
  25.7 1.9 %collective-permute-start.3 = (bf16[192,256]{1,0:T(8,128)(2,1)S(1)}, bf16[192,256]{1,0:T(8,128)(2,1)S(1)}, u32[]{:S(2)}, u32[]{:S(2)}) collective-permute-start(bf16[192,256]{1,0:T(8,128)(2,1)S(1)} %slice.13), channel_id=1, source_target_pairs={{0,8},{8,16},{16,24},{24,32},{32,40},{40,48},{48,56},{56,64},{64,7... | collective-permute-start | bytes 294920 | tf_op jit(solution)/shard_map/ppermute | solution.py:177
  27.7 2.6 %collective-permute-done.2 = bf16[256,256]{1,0:T(8,128)(2,1)S(1)} collective-permute-done((bf16[256,256]{1,0:T(8,128)(2,1)S(1)}, bf16[256,256]{1,0:T(8,128)(2,1)S(1)}, u32[]{:S(2)}, u32[]{:S(2)}) %collective-permute-start.2) | collective-permute-done | bytes 131104 | tf_op jit(solution)/shard_map/ppermute | solution.py:171
  30.3 1.8 %all-to-all-done = bf16[32,4,2048]{2,0,1:T(8,128)(2,1)S(1)} async-done(((bf16[32,4,2048]{2,0,1:T(8,128)(2,1)}), bf16[32,4,2048]{2,0,1:T(8,128)(2,1)S(1)}, u32[]{:S(2)}, u32[]{:S(2)}) %all-to-all-start) | async-done | bytes 524320 | tf_op jit(solution)/shard_map/all_to_all | solution.py:188
  32.8 1.1 broadcast_in_dim.14
  33.8 4.3 %all-to-all-start.1 = ((bf16[4,512,256]{2,1,0:T(8,128)(2,1)}), bf16[4,512,256]{2,1,0:T(8,128)(2,1)S(1)}, u32[]{:S(2)}, u32[]{:S(2)}) async-start(bf16[4,512,256]{2,1,0:T(8,128)(2,1)} %broadcast_in_dim.14), calls=%async_computation.1 | async-start | bytes 2097152 | tf_op jit(solution)/shard_map/all_to_all | solution.py:198
  38.1 11.4 %collective-permute-start.4 = (bf16[128,512]{1,0:T(8,128)(2,1)S(1)}, bf16[128,512]{1,0:T(8,128)(2,1)S(1)}, u32[]{:S(2)}, u32[]{:S(2)}) collective-permute-start(bf16[128,512]{1,0:T(8,128)(2,1)S(1)} %get-tuple-element.19), channel_id=1, source_target_pairs={{0,1},{1,0},{2,3},{3,2},{4,5},{5,4},{6,7},{7,6},{8,9},{9,8},{10,11... | collective-permute-start | bytes 393224 | tf_op jit(solution)/shard_map/ppermute | solution.py:174
  49.5 10.3 %collective-permute-done.4.far_ref = bf16[128,512]{1,0:T(8,128)(2,1)S(1)} collective-permute-done((bf16[128,512]{1,0:T(8,128)(2,1)S(1)}, bf16[128,512]{1,0:T(8,128)(2,1)S(1)}, u32[]{:S(2)}, u32[]{:S(2)}) %collective-permute-start.4) | collective-permute-done | bytes 131104 | tf_op jit(solution)/shard_map/ppermute | solution.py:174
  59.9 1.9 %collective-permute-start.5 = (bf16[2048,256]{1,0:T(8,128)(2,1)S(1)}, bf16[2048,256]{1,0:T(8,128)(2,1)S(1)}, u32[]{:S(2)}, u32[]{:S(2)}) collective-permute-start(bf16[2048,256]{1,0:T(8,128)(2,1)S(1)} %bitcast.20), channel_id=1, source_target_pairs={{0,8},{8,0},{16,24},{24,16},{32,40},{40,32},{48,56},{56,48},{64,72... | collective-permute-start | bytes 3145736 | tf_op jit(solution)/shard_map/ppermute | solution.py:171
  62.6 12.1 %collective-permute-start.6 = (bf16[128,512]{1,0:T(8,128)(2,1)}, bf16[128,512]{1,0:T(8,128)(2,1)S(1)}, u32[]{:S(2)}, u32[]{:S(2)}) collective-permute-start(bf16[128,512]{1,0:T(8,128)(2,1)} %get-tuple-element.25), channel_id=1, source_target_pairs={{0,1},{1,0},{2,3},{3,2},{4,5},{5,4},{6,7},{7,6},{8,9},{9,8},{10,11... | collective-permute-start | bytes 393224 | tf_op jit(solution)/shard_map/ppermute | solution.py:174
  75.0 5.5 %attention.2 = (bf16[128,512]{1,0:T(8,128)(2,1)S(1)}, bf16[128,512]{1,0:T(8,128)(2,1)S(1)}) custom-call(s32[384]{0:T(512)S(1)} %reshape.24.lists_ref, s32[2]{0:T(128)S(1)} %pad_add_fusion.spot_ref, bf16[128,2048]{1,0:T(8,128)(2,1)S(1)} %bitcast.18, bf16[128,512]{1,0:T(8,128)(2,1)S(1)} %collective-permute-done.4.far_ref, ...), custom_call_target="tpu_custom_call" | custom-call | flops 939524096 | bytes 4194304 | tf_op jit(solution)/shard_map/attention/pallas_call | solution.py:135
  80.5 2.4 %collective-permute-start.7 = (bf16[128,512]{1,0:T(8,128)(2,1)S(1)}, bf16[128,512]{1,0:T(8,128)(2,1)}, u32[]{:S(2)}, u32[]{:S(2)}) collective-permute-start(bf16[128,512]{1,0:T(8,128)(2,1)S(1)} %get-tuple-element.27), channel_id=1, source_target_pairs={{0,1},{1,0},{2,3},{3,2},{4,5},{5,4},{6,7},{7,6},{8,9},{9,8},{10,11... | collective-permute-start | bytes 393224 | tf_op jit(solution)/shard_map/ppermute | solution.py:174
  83.0 2.2 %collective-permute-done.6.far_ref = bf16[128,512]{1,0:T(8,128)(2,1)S(1)} collective-permute-done((bf16[128,512]{1,0:T(8,128)(2,1)}, bf16[128,512]{1,0:T(8,128)(2,1)S(1)}, u32[]{:S(2)}, u32[]{:S(2)}) %collective-permute-start.6) | collective-permute-done | bytes 131104 | tf_op jit(solution)/shard_map/ppermute | solution.py:174
  85.2 5.5 %attention.3 = (bf16[128,512]{1,0:T(8,128)(2,1)S(1)}, bf16[128,512]{1,0:T(8,128)(2,1)S(1)}) custom-call(s32[384]{0:T(512)S(1)} %reshape.26.lists_ref, s32[2]{0:T(128)S(1)} %pad_add_fusion.spot_ref, bf16[128,2048]{1,0:T(8,128)(2,1)S(1)} %bitcast.19, bf16[128,512]{1,0:T(8,128)(2,1)S(1)} %collective-permute-done.6.far_ref, ...), custom_call_target="tpu_custom_call" | custom-call | flops 939524096 | bytes 4194304 | tf_op jit(solution)/shard_map/attention/pallas_call | solution.py:135
  90.6 9.9 %collective-permute-start.8 = (bf16[128,512]{1,0:T(8,128)(2,1)S(1)}, bf16[128,512]{1,0:T(8,128)(2,1)S(1)}, u32[]{:S(2)}, u32[]{:S(2)}) collective-permute-start(bf16[128,512]{1,0:T(8,128)(2,1)S(1)} %get-tuple-element.28), channel_id=1, source_target_pairs={{0,1},{1,0},{2,3},{3,2},{4,5},{5,4},{6,7},{7,6},{8,9},{9,8},{10,11... | collective-permute-start | bytes 393224 | tf_op jit(solution)/shard_map/ppermute | solution.py:174
  100.6 11.8 %collective-permute-done.7 = bf16[128,512]{1,0:T(8,128)(2,1)} collective-permute-done((bf16[128,512]{1,0:T(8,128)(2,1)S(1)}, bf16[128,512]{1,0:T(8,128)(2,1)}, u32[]{:S(2)}, u32[]{:S(2)}) %collective-permute-start.7) | collective-permute-done | bytes 131104 | tf_op jit(solution)/shard_map/ppermute | solution.py:174
  112.4 2.2 %collective-permute-done.8 = bf16[128,512]{1,0:T(8,128)(2,1)S(1)} collective-permute-done((bf16[128,512]{1,0:T(8,128)(2,1)S(1)}, bf16[128,512]{1,0:T(8,128)(2,1)S(1)}, u32[]{:S(2)}, u32[]{:S(2)}) %collective-permute-start.8) | collective-permute-done | bytes 131104 | tf_op jit(solution)/shard_map/ppermute | solution.py:174
  114.5 1.1 maximum_select_fusion
  115.6 17.8 %all_to_all.40 = bf16[4,32,2048]{2,1,0:T(8,128)(2,1)S(1)} all-to-all(bf16[4,32,2048]{2,1,0:T(8,128)(2,1)S(1)} %maximum_select_fusion), channel_id=1, replica_groups=mesh['x'=4,'zc'=16,'y'=4,'zh'=2] {'y'}, dimensions={0} | all-to-all | bytes 1048576 | tf_op jit(solution)/shard_map/all_to_all | solution.py:219
  (27 shorter events, 3.4 us)
Async XLA Ops:
  0.0 0.7 copy-start.2
  0.7 11.0 %collective-permute-start = (bf16[64,256]{1,0:T(8,128)(2,1)S(1)}, bf16[64,256]{1,0:T(8,128)(2,1)S(1)}, u32[]{:S(2)}, u32[]{:S(2)}) collective-permute-start(bf16[64,256]{1,0:T(8,128)(2,1)S(1)} %constant_dynamic-update-slice_fusion), channel_id=1, source_target_pairs={{0,64},{8,72},{16,80},{24,88},{32,96},{40,104},{48,112},{56,120},{... | collective-permute-start | bytes 98312 | tf_op jit(solution)/shard_map/ppermute | solution.py:171
  11.7 11.5 %collective-permute-start.1 = (bf16[128,256]{1,0:T(8,128)(2,1)S(1)}, bf16[128,256]{1,0:T(8,128)(2,1)S(1)}, u32[]{:S(2)}, u32[]{:S(2)}) collective-permute-start(bf16[128,256]{1,0:T(8,128)(2,1)S(1)} %pad_maximum_fusion.2), channel_id=1, source_target_pairs={{0,32},{8,40},{16,48},{24,56},{32,0},{40,8},{48,16},{56,24},{64,96... | collective-permute-start | bytes 196616 | tf_op jit(solution)/shard_map/ppermute | solution.py:171
  18.8 13.3 %all-to-all-start = ((bf16[32,4,2048]{2,0,1:T(8,128)(2,1)}), bf16[32,4,2048]{2,0,1:T(8,128)(2,1)S(1)}, u32[]{:S(2)}, u32[]{:S(2)}) async-start(bf16[32,4,2048]{2,0,1:T(8,128)(2,1)} %bitcast.16), calls=%async_computation | async-start | bytes 1048576 | tf_op jit(solution)/shard_map/all_to_all | solution.py:188
  23.3 2.4 %copy-start = (bf16[256,128]{1,0:T(8,128)(2,1)S(1)}, bf16[256,128]{1,0:T(8,128)(2,1)}, u32[]{:S(2)}) copy-start(bf16[256,128]{1,0:T(8,128)(2,1)} %param.9) | copy-start | bytes 196612
  23.3 2.4 %copy-start.1 = (bf16[256,128]{1,0:T(8,128)(2,1)S(1)}, bf16[256,128]{1,0:T(8,128)(2,1)}, u32[]{:S(2)}) copy-start(bf16[256,128]{1,0:T(8,128)(2,1)} %param.10) | copy-start | bytes 196612
  23.3 7.0 %collective-permute-start.2 = (bf16[256,256]{1,0:T(8,128)(2,1)S(1)}, bf16[256,256]{1,0:T(8,128)(2,1)S(1)}, u32[]{:S(2)}, u32[]{:S(2)}) collective-permute-start(bf16[256,256]{1,0:T(8,128)(2,1)S(1)} %pad_maximum_fusion.1), channel_id=1, source_target_pairs={{0,16},{8,24},{16,0},{24,8},{32,48},{40,56},{48,32},{56,40},{64,80... | collective-permute-start | bytes 393224 | tf_op jit(solution)/shard_map/ppermute | solution.py:171
  25.7 7.0 %collective-permute-start.3 = (bf16[192,256]{1,0:T(8,128)(2,1)S(1)}, bf16[192,256]{1,0:T(8,128)(2,1)S(1)}, u32[]{:S(2)}, u32[]{:S(2)}) collective-permute-start(bf16[192,256]{1,0:T(8,128)(2,1)S(1)} %slice.13), channel_id=1, source_target_pairs={{0,8},{8,16},{16,24},{24,32},{32,40},{40,48},{48,56},{56,64},{64,7... | collective-permute-start | bytes 294920 | tf_op jit(solution)/shard_map/ppermute | solution.py:177
  33.8 26.1 %all-to-all-start.1 = ((bf16[4,512,256]{2,1,0:T(8,128)(2,1)}), bf16[4,512,256]{2,1,0:T(8,128)(2,1)S(1)}, u32[]{:S(2)}, u32[]{:S(2)}) async-start(bf16[4,512,256]{2,1,0:T(8,128)(2,1)} %broadcast_in_dim.14), calls=%async_computation.1 | async-start | bytes 2097152 | tf_op jit(solution)/shard_map/all_to_all | solution.py:198
  38.1 21.8 %collective-permute-start.4 = (bf16[128,512]{1,0:T(8,128)(2,1)S(1)}, bf16[128,512]{1,0:T(8,128)(2,1)S(1)}, u32[]{:S(2)}, u32[]{:S(2)}) collective-permute-start(bf16[128,512]{1,0:T(8,128)(2,1)S(1)} %get-tuple-element.19), channel_id=1, source_target_pairs={{0,1},{1,0},{2,3},{3,2},{4,5},{5,4},{6,7},{7,6},{8,9},{9,8},{10,11... | collective-permute-start | bytes 393224 | tf_op jit(solution)/shard_map/ppermute | solution.py:174
  59.9 15.1 %collective-permute-start.5 = (bf16[2048,256]{1,0:T(8,128)(2,1)S(1)}, bf16[2048,256]{1,0:T(8,128)(2,1)S(1)}, u32[]{:S(2)}, u32[]{:S(2)}) collective-permute-start(bf16[2048,256]{1,0:T(8,128)(2,1)S(1)} %bitcast.20), channel_id=1, source_target_pairs={{0,8},{8,0},{16,24},{24,16},{32,40},{40,32},{48,56},{56,48},{64,72... | collective-permute-start | bytes 3145736 | tf_op jit(solution)/shard_map/ppermute | solution.py:171
  61.8 0.7 copy-start.3
  62.6 22.5 %collective-permute-start.6 = (bf16[128,512]{1,0:T(8,128)(2,1)}, bf16[128,512]{1,0:T(8,128)(2,1)S(1)}, u32[]{:S(2)}, u32[]{:S(2)}) collective-permute-start(bf16[128,512]{1,0:T(8,128)(2,1)} %get-tuple-element.25), channel_id=1, source_target_pairs={{0,1},{1,0},{2,3},{3,2},{4,5},{5,4},{6,7},{7,6},{8,9},{9,8},{10,11... | collective-permute-start | bytes 393224 | tf_op jit(solution)/shard_map/ppermute | solution.py:174
  80.5 31.9 %collective-permute-start.7 = (bf16[128,512]{1,0:T(8,128)(2,1)S(1)}, bf16[128,512]{1,0:T(8,128)(2,1)}, u32[]{:S(2)}, u32[]{:S(2)}) collective-permute-start(bf16[128,512]{1,0:T(8,128)(2,1)S(1)} %get-tuple-element.27), channel_id=1, source_target_pairs={{0,1},{1,0},{2,3},{3,2},{4,5},{5,4},{6,7},{7,6},{8,9},{9,8},{10,11... | collective-permute-start | bytes 393224 | tf_op jit(solution)/shard_map/ppermute | solution.py:174
  90.6 23.9 %collective-permute-start.8 = (bf16[128,512]{1,0:T(8,128)(2,1)S(1)}, bf16[128,512]{1,0:T(8,128)(2,1)S(1)}, u32[]{:S(2)}, u32[]{:S(2)}) collective-permute-start(bf16[128,512]{1,0:T(8,128)(2,1)S(1)} %get-tuple-element.28), channel_id=1, source_target_pairs={{0,1},{1,0},{2,3},{3,2},{4,5},{5,4},{6,7},{7,6},{8,9},{9,8},{10,11... | collective-permute-start | bytes 393224 | tf_op jit(solution)/shard_map/ppermute | solution.py:174

commit v2 on v1

--- a/solution.py
+++ b/solution.py
@@ -13,7 +13,6 @@
 NV = 12
 WIN = 4
 X, ZL, CORE = 4, 8, 2
-CHUNKS = 2
 NEG = -1e30
 HEADS_A_STEP = 4
 
@@ -139,7 +138,7 @@
             grid=(heads // HEADS_A_STEP,),
             in_specs=[
                 pl.BlockSpec((tokens, HEADS_A_STEP * DH), lambda h, _, spot: (0, (spot[1] * group + start) // HEADS_A_STEP + h)),
-                pl.BlockSpec((tokens, HEADS_A_STEP * DH), lambda h, *_: (0, h)),
+                pl.BlockSpec((tokens, HEADS_A_STEP * DH), lambda h, *_: (0, start // HEADS_A_STEP + h)),
                 whole,
                 whole,
                 *[pl.BlockSpec(memory_space=pl.ANY)] * len(pieces),
@@ -165,7 +164,6 @@
     count = X * ZL * CORE
     group = block_lists.shape[0]
     seq, side = lax.axis_index(("x", "zc")), lax.axis_index("zh")
-    heads = group // CHUNKS
 
     def send(array, target):
         return lax.ppermute(array, ("x", "zc"), [(i, target(i)) for i in range(count)])
@@ -174,9 +172,7 @@
         return lax.ppermute(array, "zh", [(0, 1), (1, 0)])
 
     slab = jnp.concatenate([slab_keys, slab_values], axis=1)
-    halo = lax.ppermute(
-        slab[-(WIN - 1) * BLOCK :], ("x", "zc"), [(i, i + 1) for i in range(count - 1)]
-    )
+    tail = slab[-(WIN - 1) * BLOCK :]
 
     held = jnp.concatenate([cache_keys, cache_values], axis=1)
     order = [0]
@@ -186,18 +182,14 @@
         if bit == 4:
             queries, held = lax.optimization_barrier((queries, held))
             near = lax.all_to_all(queries, "y", split_axis=1, concat_axis=0, tiled=True)
-    leaving = [
-        lax.dynamic_slice_in_dim(
-            near, ((1 - side) * group + chunk * heads) * DH, heads * DH, axis=1
-        )
-        for chunk in range(CHUNKS)
-    ]
-    leaving, held, halo = lax.optimization_barrier((leaving, held, halo))
-    far = [over_side(part) for part in leaving]
+    leaving = lax.dynamic_slice_in_dim(near, (1 - side) * group * DH, group * DH, axis=1)
+    leaving, held, tail = lax.optimization_barrier((leaving, held, tail))
+    halo = lax.ppermute(tail, ("x", "zc"), [(i, i + 1) for i in range(count - 1)])
+    far = over_side(leaving)
     copies = jnp.broadcast_to(held[None], (X, *held.shape))
     along_x = lax.all_to_all(copies, "x", split_axis=0, concat_axis=0, tiled=True)
     along_x = along_x.reshape(-1, 2 * DH)
-    far[0], along_x = lax.optimization_barrier((far[0], along_x))
+    far, halo, along_x = lax.optimization_barrier((far, halo, along_x))
     pieces = [along_x, send(along_x, lambda i: i ^ 1)]
 
     place = [order.index(p) for p in range(ZL)]
@@ -208,15 +200,12 @@
     lists = (block_core ^ own_core) * (X * ZL) + block_x * ZL + z_place
 
     spot = jnp.stack([seq, side])
-    mine, back = [], []
-    for chunk in range(CHUNKS):
-        here, theirs = attention(lists, spot, near, far[chunk], halo, slab, pieces, chunk * heads, heads)
-        mine.append(here)
-        back.append(over_side(theirs))
-    both = jnp.where(
-        side == 0, jnp.concatenate(mine + back, axis=1), jnp.concatenate(back + mine, axis=1)
-    )
-    return lax.all_to_all(both, "y", split_axis=0, concat_axis=1, tiled=True)
+    mine, theirs = attention(lists, spot, near, far, halo, slab, pieces, 0, group)
+    rows = queries.shape[0]
+    halves = [half.reshape(-1, 1, rows, group * DH) for half in (mine, theirs)]
+    both = jnp.where(side == 0, jnp.concatenate(halves, axis=1), jnp.concatenate(halves[::-1], axis=1))
+    both = both.reshape(-1, group * DH)
+    return lax.all_to_all(both, ("y", "zh"), split_axis=0, concat_axis=1, tiled=True)
 
 
 def solution(mesh):

time: 135 us -> 127 us (0.941)
  the two profiles are of different devices: /device:TPU:32 before, /device:TPU:67 now
where the time goes in v2:
time: 127 us
  starting transfers between devices  55.8 us (44%)
  blocking collectives  41.7 us (33%)
  waiting for transfers between devices  13 us (10%)
  Pallas kernels  10.4 us (8%)
  local copies, waits for them, and re-layouts  5.36 us (4%)
    all_to_all x1, blocking collectives, per_device(): lax.all_to_all(both, ('y', 'zh'), split_axis=0, concat_axis=1, tiled=True)  41.7 us
    ppermute x4, starting transfers between devices, send(): lax.ppermute(array, ('x', 'zc'), [(i, target(i)) for i in range(count)])  27.1 us
    ppermute x1, starting transfers between devices, over_side(): return lax.ppermute(array, 'zh', [(0, 1), (1, 0)])  12.8 us
    pallas_call x1, Pallas kernels, attention(): pl.pallas_call(functools.partial(attention_kernel, pieces=len(pieces), bl...  10.4 us
    ppermute x1, waiting for transfers between devices, per_device(): lax.ppermute(tail, ('x', 'zc'), [(i, i + 1) for i in range(count - 1)])  7.41 us
    ppermute x1, starting transfers between devices, per_device(): lax.ppermute(tail, ('x', 'zc'), [(i, i + 1) for i in range(count - 1)])  7.38 us
    ppermute x4, waiting for transfers between devices, send(): lax.ppermute(array, ('x', 'zc'), [(i, target(i)) for i in range(count)])  5.12 us
    all_to_all x1, starting transfers between devices, per_device(): lax.all_to_all(copies, 'x', split_axis=0, concat_axis=0, tiled=True)  4.26 us
  transfers between devices with their start and end apart: 8, of which 5 were waited for; matrix products, arithmetic and copies ran while one was open for 2% of the time, Pallas kernels for 0%

profile of v2, /device:TPU:67, one launch (start us, length us, event | category | flops | bytes accessed | tf_op | source)
XLA Modules:
  0.0 126.7 jit_solution(1142171764863379168)
XLA Ops:
  0.0 0.7 constant_dynamic-update-slice_fusion.1
  0.7 8.8 %collective-permute-start = (bf16[64,256]{1,0:T(8,128)(2,1)S(1)}, bf16[64,256]{1,0:T(8,128)(2,1)S(1)}, u32[]{:S(2)}, u32[]{:S(2)}) collective-permute-start(bf16[64,256]{1,0:T(8,128)(2,1)S(1)} %constant_dynamic-update-slice_fusion), channel_id=1, source_target_pairs={{0,64},{8,72},{16,80},{24,88},{32,96},{40,104},{48,112},{56,120},{... | collective-permute-start | bytes 98312 | tf_op jit(solution)/shard_map/ppermute | solution.py:169
  9.6 1.3 %collective-permute-done = bf16[64,256]{1,0:T(8,128)(2,1)S(1)} collective-permute-done((bf16[64,256]{1,0:T(8,128)(2,1)S(1)}, bf16[64,256]{1,0:T(8,128)(2,1)S(1)}, u32[]{:S(2)}, u32[]{:S(2)}) %collective-permute-start) | collective-permute-done | bytes 32800 | tf_op jit(solution)/shard_map/ppermute | solution.py:169
  10.9 1.9 %collective-permute-start.1 = (bf16[128,256]{1,0:T(8,128)(2,1)S(1)}, bf16[128,256]{1,0:T(8,128)(2,1)S(1)}, u32[]{:S(2)}, u32[]{:S(2)}) collective-permute-start(bf16[128,256]{1,0:T(8,128)(2,1)S(1)} %pad_maximum_fusion.2), channel_id=1, source_target_pairs={{0,32},{8,40},{16,48},{24,56},{32,0},{40,8},{48,16},{56,24},{64,96... | collective-permute-start | bytes 196616 | tf_op jit(solution)/shard_map/ppermute | solution.py:169
  12.8 1.9 %copy.22 = bf16[4,4,8,2048]{3,2,0,1:T(8,128)(2,1)} copy(bf16[4,4,8,2048]{3,2,1,0:T(8,128)(2,1)} %bitcast.28) | data formatting | bytes 1048576 | tf_op jit(solution)/shard_map/all_to_all | solution.py:184
  14.7 4.2 %all-to-all-start = ((bf16[32,4,2048]{2,0,1:T(8,128)(2,1)}), bf16[32,4,2048]{2,0,1:T(8,128)(2,1)S(1)}, u32[]{:S(2)}, u32[]{:S(2)}) async-start(bf16[32,4,2048]{2,0,1:T(8,128)(2,1)} %bitcast.19), calls=%async_computation | async-start | bytes 1048576 | tf_op jit(solution)/shard_map/all_to_all | solution.py:184
  18.9 4.2 %collective-permute-start.2 = (bf16[256,256]{1,0:T(8,128)(2,1)S(1)}, bf16[256,256]{1,0:T(8,128)(2,1)S(1)}, u32[]{:S(2)}, u32[]{:S(2)}) collective-permute-start(bf16[256,256]{1,0:T(8,128)(2,1)S(1)} %pad_maximum_fusion.1), channel_id=1, source_target_pairs={{0,16},{8,24},{16,0},{24,8},{32,48},{40,56},{48,32},{56,40},{64,80... | collective-permute-start | bytes 393224 | tf_op jit(solution)/shard_map/ppermute | solution.py:169
  23.2 2.5 %collective-permute-done.2 = bf16[256,256]{1,0:T(8,128)(2,1)S(1)} collective-permute-done((bf16[256,256]{1,0:T(8,128)(2,1)S(1)}, bf16[256,256]{1,0:T(8,128)(2,1)S(1)}, u32[]{:S(2)}, u32[]{:S(2)}) %collective-permute-start.2) | collective-permute-done | bytes 131104 | tf_op jit(solution)/shard_map/ppermute | solution.py:169
  25.7 0.5 all-to-all-done
  26.3 1.1 broadcast_in_dim.14
  27.3 4.3 %all-to-all-start.1 = ((bf16[4,512,256]{2,1,0:T(8,128)(2,1)}), bf16[4,512,256]{2,1,0:T(8,128)(2,1)S(1)}, u32[]{:S(2)}, u32[]{:S(2)}) async-start(bf16[4,512,256]{2,1,0:T(8,128)(2,1)} %broadcast_in_dim.14), calls=%async_computation.1 | async-start | bytes 2097152 | tf_op jit(solution)/shard_map/all_to_all | solution.py:190
  31.6 12.8 %collective-permute-start.3 = (bf16[128,1024]{1,0:T(8,128)(2,1)S(1)}, bf16[128,1024]{1,0:T(8,128)(2,1)S(1)}, u32[]{:S(2)}, u32[]{:S(2)}) collective-permute-start(bf16[128,1024]{1,0:T(8,128)(2,1)S(1)} %constant_dynamic-slice_fusion), channel_id=1, source_target_pairs={{0,1},{1,0},{2,3},{3,2},{4,5},{5,4},{6,7},{7,6},{8,9},{9,8},{10,11... | collective-permute-start | bytes 786440 | tf_op jit(solution)/shard_map/ppermute | solution.py:172
  44.4 7.4 %collective-permute-start.4 = (bf16[192,256]{1,0:T(8,128)(2,1)S(1)}, bf16[192,256]{1,0:T(8,128)(2,1)S(1)}, u32[]{:S(2)}, u32[]{:S(2)}) collective-permute-start(bf16[192,256]{1,0:T(8,128)(2,1)S(1)} %slice.4), channel_id=1, source_target_pairs={{0,8},{8,16},{16,24},{24,32},{32,40},{40,48},{48,56},{56,64},{64,7... | collective-permute-start | bytes 294920 | tf_op jit(solution)/shard_map/ppermute | solution.py:187
  51.8 7.4 %collective-permute-done.4.halo_ref = bf16[192,256]{1,0:T(8,128)(2,1)S(1)} collective-permute-done((bf16[192,256]{1,0:T(8,128)(2,1)S(1)}, bf16[192,256]{1,0:T(8,128)(2,1)S(1)}, u32[]{:S(2)}, u32[]{:S(2)}) %collective-permute-start.4) | collective-permute-done | bytes 98336 | tf_op jit(solution)/shard_map/ppermute | solution.py:187
  59.2 12.2 %collective-permute-start.5 = (bf16[2048,256]{1,0:T(8,128)(2,1)S(1)}, bf16[2048,256]{1,0:T(8,128)(2,1)S(1)}, u32[]{:S(2)}, u32[]{:S(2)}) collective-permute-start(bf16[2048,256]{1,0:T(8,128)(2,1)S(1)} %bitcast.22), channel_id=1, source_target_pairs={{0,8},{8,0},{16,24},{24,16},{32,40},{40,32},{48,56},{56,48},{64,72... | collective-permute-start | bytes 3145736 | tf_op jit(solution)/shard_map/ppermute | solution.py:169
  71.5 0.7 copy-done.3
  72.2 0.1 fusion.3
  72.2 0.1 reshape.26.lists_ref
  72.3 0.1 pad_add_fusion.spot_ref
  72.4 1.3 %collective-permute-done.5.rest_1_ = bf16[2048,256]{1,0:T(8,128)(2,1)S(1)} collective-permute-done((bf16[2048,256]{1,0:T(8,128)(2,1)S(1)}, bf16[2048,256]{1,0:T(8,128)(2,1)S(1)}, u32[]{:S(2)}, u32[]{:S(2)}) %collective-permute-start.5) | collective-permute-done | bytes 1048608 | tf_op jit(solution)/shard_map/ppermute | solution.py:169
  73.7 10.4 %attention.1 = (bf16[128,1024]{1,0:T(8,128)(2,1)S(1)}, bf16[128,1024]{1,0:T(8,128)(2,1)S(1)}) custom-call(s32[768]{0:T(1024)S(1)} %reshape.26.lists_ref, s32[2]{0:T(128)S(1)} %pad_add_fusion.spot_ref, bf16[128,2048]{1,0:T(8,128)(2,1)S(1)} %bitcast.21, bf16[128,1024]{1,0:T(8,128)(2,1)S(1)} %collective-permute-done.3.far_ref, ...), custom_call_target="tpu_custom_call" | custom-call | flops 1879048192 | bytes 4194304 | tf_op jit(solution)/shard_map/attention/pallas_call | solution.py:134
  84.1 0.1 maximum_select_fusion
  84.2 41.7 %all_to_all.40 = bf16[8,32,1024]{2,1,0:T(8,128)(2,1)S(1)} all-to-all(bf16[8,32,1024]{2,1,0:T(8,128)(2,1)S(1)} %bitcast.26), channel_id=1, replica_groups=mesh['x'=4,'zc'=16,'y'=4,'zh'=2] {'y','zh'}, dimensions={0} | all-to-all | bytes 1048576 | tf_op jit(solution)/shard_map/all_to_all | solution.py:208
  125.9 0.8 copy.20
  (18 shorter events, 0.1 us)
Async XLA Ops:
  0.0 0.7 copy-start.2
  0.7 10.1 %collective-permute-start = (bf16[64,256]{1,0:T(8,128)(2,1)S(1)}, bf16[64,256]{1,0:T(8,128)(2,1)S(1)}, u32[]{:S(2)}, u32[]{:S(2)}) collective-permute-start(bf16[64,256]{1,0:T(8,128)(2,1)S(1)} %constant_dynamic-update-slice_fusion), channel_id=1, source_target_pairs={{0,64},{8,72},{16,80},{24,88},{32,96},{40,104},{48,112},{56,120},{... | collective-permute-start | bytes 98312 | tf_op jit(solution)/shard_map/ppermute | solution.py:169
  10.9 8.0 %collective-permute-start.1 = (bf16[128,256]{1,0:T(8,128)(2,1)S(1)}, bf16[128,256]{1,0:T(8,128)(2,1)S(1)}, u32[]{:S(2)}, u32[]{:S(2)}) collective-permute-start(bf16[128,256]{1,0:T(8,128)(2,1)S(1)} %pad_maximum_fusion.2), channel_id=1, source_target_pairs={{0,32},{8,40},{16,48},{24,56},{32,0},{40,8},{48,16},{56,24},{64,96... | collective-permute-start | bytes 196616 | tf_op jit(solution)/shard_map/ppermute | solution.py:169
  14.7 11.6 %all-to-all-start = ((bf16[32,4,2048]{2,0,1:T(8,128)(2,1)}), bf16[32,4,2048]{2,0,1:T(8,128)(2,1)S(1)}, u32[]{:S(2)}, u32[]{:S(2)}) async-start(bf16[32,4,2048]{2,0,1:T(8,128)(2,1)} %bitcast.19), calls=%async_computation | async-start | bytes 1048576 | tf_op jit(solution)/shard_map/all_to_all | solution.py:184
  18.9 4.2 %copy-start = (bf16[256,128]{1,0:T(8,128)(2,1)S(1)}, bf16[256,128]{1,0:T(8,128)(2,1)}, u32[]{:S(2)}) copy-start(bf16[256,128]{1,0:T(8,128)(2,1)} %param.9) | copy-start | bytes 196612
  18.9 4.2 %copy-start.1 = (bf16[256,128]{1,0:T(8,128)(2,1)S(1)}, bf16[256,128]{1,0:T(8,128)(2,1)}, u32[]{:S(2)}) copy-start(bf16[256,128]{1,0:T(8,128)(2,1)} %param.10) | copy-start | bytes 196612
  18.9 6.8 %collective-permute-start.2 = (bf16[256,256]{1,0:T(8,128)(2,1)S(1)}, bf16[256,256]{1,0:T(8,128)(2,1)S(1)}, u32[]{:S(2)}, u32[]{:S(2)}) collective-permute-start(bf16[256,256]{1,0:T(8,128)(2,1)S(1)} %pad_maximum_fusion.1), channel_id=1, source_target_pairs={{0,16},{8,24},{16,0},{24,8},{32,48},{40,56},{48,32},{56,40},{64,80... | collective-permute-start | bytes 393224 | tf_op jit(solution)/shard_map/ppermute | solution.py:169
  27.3 31.9 %all-to-all-start.1 = ((bf16[4,512,256]{2,1,0:T(8,128)(2,1)}), bf16[4,512,256]{2,1,0:T(8,128)(2,1)S(1)}, u32[]{:S(2)}, u32[]{:S(2)}) async-start(bf16[4,512,256]{2,1,0:T(8,128)(2,1)} %broadcast_in_dim.14), calls=%async_computation.1 | async-start | bytes 2097152 | tf_op jit(solution)/shard_map/all_to_all | solution.py:190
  31.6 27.6 %collective-permute-start.3 = (bf16[128,1024]{1,0:T(8,128)(2,1)S(1)}, bf16[128,1024]{1,0:T(8,128)(2,1)S(1)}, u32[]{:S(2)}, u32[]{:S(2)}) collective-permute-start(bf16[128,1024]{1,0:T(8,128)(2,1)S(1)} %constant_dynamic-slice_fusion), channel_id=1, source_target_pairs={{0,1},{1,0},{2,3},{3,2},{4,5},{5,4},{6,7},{7,6},{8,9},{9,8},{10,11... | collective-permute-start | bytes 786440 | tf_op jit(solution)/shard_map/ppermute | solution.py:172
  44.4 14.8 %collective-permute-start.4 = (bf16[192,256]{1,0:T(8,128)(2,1)S(1)}, bf16[192,256]{1,0:T(8,128)(2,1)S(1)}, u32[]{:S(2)}, u32[]{:S(2)}) collective-permute-start(bf16[192,256]{1,0:T(8,128)(2,1)S(1)} %slice.4), channel_id=1, source_target_pairs={{0,8},{8,16},{16,24},{24,32},{32,40},{40,48},{48,56},{56,64},{64,7... | collective-permute-start | bytes 294920 | tf_op jit(solution)/shard_map/ppermute | solution.py:187
  59.2 14.5 %collective-permute-start.5 = (bf16[2048,256]{1,0:T(8,128)(2,1)S(1)}, bf16[2048,256]{1,0:T(8,128)(2,1)S(1)}, u32[]{:S(2)}, u32[]{:S(2)}) collective-permute-start(bf16[2048,256]{1,0:T(8,128)(2,1)S(1)} %bitcast.22), channel_id=1, source_target_pairs={{0,8},{8,0},{16,24},{24,16},{32,40},{40,32},{48,56},{56,48},{64,72... | collective-permute-start | bytes 3145736 | tf_op jit(solution)/shard_map/ppermute | solution.py:169
  71.4 0.7 copy-start.3

commit v3 on v2

--- a/solution.py
+++ b/solution.py
@@ -184,20 +184,19 @@
             near = lax.all_to_all(queries, "y", split_axis=1, concat_axis=0, tiled=True)
     leaving = lax.dynamic_slice_in_dim(near, (1 - side) * group * DH, group * DH, axis=1)
     leaving, held, tail = lax.optimization_barrier((leaving, held, tail))
+    far = over_side(leaving)
     halo = lax.ppermute(tail, ("x", "zc"), [(i, i + 1) for i in range(count - 1)])
-    far = over_side(leaving)
-    copies = jnp.broadcast_to(held[None], (X, *held.shape))
-    along_x = lax.all_to_all(copies, "x", split_axis=0, concat_axis=0, tiled=True)
-    along_x = along_x.reshape(-1, 2 * DH)
-    far, halo, along_x = lax.optimization_barrier((far, halo, along_x))
-    pieces = [along_x, send(along_x, lambda i: i ^ 1)]
+    shifted = [send(held, lambda i: (i + k * ZL * CORE) % count) for k in range(1, X)]
+    far, halo, shifted = lax.optimization_barrier((far, halo, shifted))
+    along_x = [held, *shifted]
+    pieces = along_x + [send(piece, lambda i: i ^ 1) for piece in along_x]
 
     place = [order.index(p) for p in range(ZL)]
     block_x, block_z, block_core = block_lists // (ZL * CORE), block_lists // CORE % ZL, block_lists % CORE
-    own_z, own_core = seq // CORE % ZL, seq % CORE
+    own_x, own_z, own_core = seq // (ZL * CORE), seq // CORE % ZL, seq % CORE
     z_bits = block_z ^ own_z
     z_place = sum(jnp.where((z_bits & bit) != 0, place[bit], 0) for bit in (4, 2, 1))
-    lists = (block_core ^ own_core) * (X * ZL) + block_x * ZL + z_place
+    lists = (block_core ^ own_core) * (X * ZL) + (own_x - block_x) % X * ZL + z_place
 
     spot = jnp.stack([seq, side])
     mine, theirs = attention(lists, spot, near, far, halo, slab, pieces, 0, group)

time: 127 us -> 131 us (1.031)
  the two profiles are of different devices: /device:TPU:67 before, /device:TPU:34 now
where the time goes in v3:
time: 131 us
  starting transfers between devices  52.9 us (40%)
  blocking collectives  45.4 us (35%)
  waiting for transfers between devices  17.8 us (14%)
  Pallas kernels  10.5 us (8%)
  local copies, waits for them, and re-layouts  3.63 us (3%)
    all_to_all x1, blocking collectives, per_device(): lax.all_to_all(both, ('y', 'zh'), split_axis=0, concat_axis=1, tiled=True)  45.4 us
    ppermute x10, starting transfers between devices, send(): lax.ppermute(array, ('x', 'zc'), [(i, target(i)) for i in range(count)])  35.5 us
    ppermute x1, starting transfers between devices, over_side(): return lax.ppermute(array, 'zh', [(0, 1), (1, 0)])  11 us
    pallas_call x1, Pallas kernels, attention(): pl.pallas_call(functools.partial(attention_kernel, pieces=len(pieces), bl...  10.5 us
    ppermute x1, waiting for transfers between devices, per_device(): lax.ppermute(tail, ('x', 'zc'), [(i, i + 1) for i in range(count - 1)])  8.51 us
    ppermute x10, waiting for transfers between devices, send(): lax.ppermute(array, ('x', 'zc'), [(i, target(i)) for i in range(count)])  7.49 us
    all_to_all x1, starting transfers between devices, per_device(): near = lax.all_to_all(queries, 'y', split_axis=1, concat_axis=0, tiled=True)  4.46 us
  transfers between devices with their start and end apart: 13, of which 5 were waited for; matrix products, arithmetic and copies ran while one was open for 2% of the time, Pallas kernels for 0%

profile of v3, /device:TPU:34, one launch (start us, length us, event | category | flops | bytes accessed | tf_op | source)
XLA Modules:
  0.0 130.8 jit_solution(15009219507214367375)
XLA Ops:
  0.0 0.7 constant_dynamic-update-slice_fusion.1
  0.7 9.1 %collective-permute-start = (bf16[64,256]{1,0:T(8,128)(2,1)S(1)}, bf16[64,256]{1,0:T(8,128)(2,1)S(1)}, u32[]{:S(2)}, u32[]{:S(2)}) collective-permute-start(bf16[64,256]{1,0:T(8,128)(2,1)S(1)} %constant_dynamic-update-slice_fusion), channel_id=1, source_target_pairs={{0,64},{8,72},{16,80},{24,88},{32,96},{40,104},{48,112},{56,120},{... | collective-permute-start | bytes 98312 | tf_op jit(solution)/shard_map/ppermute | solution.py:169
  9.9 1.9 %collective-permute-done = bf16[64,256]{1,0:T(8,128)(2,1)S(1)} collective-permute-done((bf16[64,256]{1,0:T(8,128)(2,1)S(1)}, bf16[64,256]{1,0:T(8,128)(2,1)S(1)}, u32[]{:S(2)}, u32[]{:S(2)}) %collective-permute-start) | collective-permute-done | bytes 32800 | tf_op jit(solution)/shard_map/ppermute | solution.py:169
  11.7 5.2 %collective-permute-start.1 = (bf16[128,256]{1,0:T(8,128)(2,1)S(1)}, bf16[128,256]{1,0:T(8,128)(2,1)S(1)}, u32[]{:S(2)}, u32[]{:S(2)}) collective-permute-start(bf16[128,256]{1,0:T(8,128)(2,1)S(1)} %pad_maximum_fusion.2), channel_id=1, source_target_pairs={{0,32},{8,40},{16,48},{24,56},{32,0},{40,8},{48,16},{56,24},{64,96... | collective-permute-start | bytes 196616 | tf_op jit(solution)/shard_map/ppermute | solution.py:169
  16.9 1.9 %copy.22 = bf16[4,4,8,2048]{3,2,0,1:T(8,128)(2,1)} copy(bf16[4,4,8,2048]{3,2,1,0:T(8,128)(2,1)} %bitcast.25) | data formatting | bytes 1048576 | tf_op jit(solution)/shard_map/all_to_all | solution.py:184
  18.8 4.5 %all-to-all-start = ((bf16[32,4,2048]{2,0,1:T(8,128)(2,1)}), bf16[32,4,2048]{2,0,1:T(8,128)(2,1)S(1)}, u32[]{:S(2)}, u32[]{:S(2)}) async-start(bf16[32,4,2048]{2,0,1:T(8,128)(2,1)} %bitcast.18), calls=%async_computation | async-start | bytes 1048576 | tf_op jit(solution)/shard_map/all_to_all | solution.py:184
  23.3 2.1 %collective-permute-start.2 = (bf16[256,256]{1,0:T(8,128)(2,1)S(1)}, bf16[256,256]{1,0:T(8,128)(2,1)S(1)}, u32[]{:S(2)}, u32[]{:S(2)}) collective-permute-start(bf16[256,256]{1,0:T(8,128)(2,1)S(1)} %pad_maximum_fusion.1), channel_id=1, source_target_pairs={{0,16},{8,24},{16,0},{24,8},{32,48},{40,56},{48,32},{56,40},{64,80... | collective-permute-start | bytes 393224 | tf_op jit(solution)/shard_map/ppermute | solution.py:169
  25.5 4.7 %collective-permute-done.2 = bf16[256,256]{1,0:T(8,128)(2,1)S(1)} collective-permute-done((bf16[256,256]{1,0:T(8,128)(2,1)S(1)}, bf16[256,256]{1,0:T(8,128)(2,1)S(1)}, u32[]{:S(2)}, u32[]{:S(2)}) %collective-permute-start.2) | collective-permute-done | bytes 131104 | tf_op jit(solution)/shard_map/ppermute | solution.py:169
  30.3 1.8 %all-to-all-done = bf16[32,4,2048]{2,0,1:T(8,128)(2,1)S(1)} async-done(((bf16[32,4,2048]{2,0,1:T(8,128)(2,1)}), bf16[32,4,2048]{2,0,1:T(8,128)(2,1)S(1)}, u32[]{:S(2)}, u32[]{:S(2)}) %all-to-all-start) | async-done | bytes 524320 | tf_op jit(solution)/shard_map/all_to_all | solution.py:184
  32.1 11.0 %collective-permute-start.3 = (bf16[128,1024]{1,0:T(8,128)(2,1)S(1)}, bf16[128,1024]{1,0:T(8,128)(2,1)S(1)}, u32[]{:S(2)}, u32[]{:S(2)}) collective-permute-start(bf16[128,1024]{1,0:T(8,128)(2,1)S(1)} %constant_dynamic-slice_fusion), channel_id=1, source_target_pairs={{0,1},{1,0},{2,3},{3,2},{4,5},{5,4},{6,7},{7,6},{8,9},{9,8},{10,11... | collective-permute-start | bytes 786440 | tf_op jit(solution)/shard_map/ppermute | solution.py:172
  43.1 2.4 %collective-permute-start.7 = (bf16[512,256]{1,0:T(8,128)(2,1)S(1)}, bf16[512,256]{1,0:T(8,128)(2,1)S(1)}, u32[]{:S(2)}, u32[]{:S(2)}) collective-permute-start(bf16[512,256]{1,0:T(8,128)(2,1)S(1)} %pad_maximum_fusion.rest_0_), channel_id=1, source_target_pairs={{0,384},{8,392},{16,400},{24,408},{32,416},{40,424},{48,432},{56,4... | collective-permute-start | bytes 786440 | tf_op jit(solution)/shard_map/ppermute | solution.py:169
  45.6 4.3 %collective-permute-start.6 = (bf16[512,256]{1,0:T(8,128)(2,1)S(1)}, bf16[512,256]{1,0:T(8,128)(2,1)S(1)}, u32[]{:S(2)}, u32[]{:S(2)}) collective-permute-start(bf16[512,256]{1,0:T(8,128)(2,1)S(1)} %pad_maximum_fusion.rest_0_), channel_id=1, source_target_pairs={{0,256},{8,264},{16,272},{24,280},{32,288},{40,296},{48,304},{56,3... | collective-permute-start | bytes 786440 | tf_op jit(solution)/shard_map/ppermute | solution.py:169
  49.9 3.7 %collective-permute-start.5 = (bf16[512,256]{1,0:T(8,128)(2,1)S(1)}, bf16[512,256]{1,0:T(8,128)(2,1)S(1)}, u32[]{:S(2)}, u32[]{:S(2)}) collective-permute-start(bf16[512,256]{1,0:T(8,128)(2,1)S(1)} %pad_maximum_fusion.rest_0_), channel_id=1, source_target_pairs={{0,128},{8,136},{16,144},{24,152},{32,160},{40,168},{48,176},{56,1... | collective-permute-start | bytes 786440 | tf_op jit(solution)/shard_map/ppermute | solution.py:169
  53.6 1.9 %collective-permute-start.4 = (bf16[192,256]{1,0:T(8,128)(2,1)S(1)}, bf16[192,256]{1,0:T(8,128)(2,1)S(1)}, u32[]{:S(2)}, u32[]{:S(2)}) collective-permute-start(bf16[192,256]{1,0:T(8,128)(2,1)S(1)} %slice.4), channel_id=1, source_target_pairs={{0,8},{8,16},{16,24},{24,32},{32,40},{40,48},{48,56},{56,64},{64,7... | collective-permute-start | bytes 294920 | tf_op jit(solution)/shard_map/ppermute | solution.py:188
  55.6 8.5 %collective-permute-done.4.halo_ref = bf16[192,256]{1,0:T(8,128)(2,1)S(1)} collective-permute-done((bf16[192,256]{1,0:T(8,128)(2,1)S(1)}, bf16[192,256]{1,0:T(8,128)(2,1)S(1)}, u32[]{:S(2)}, u32[]{:S(2)}) %collective-permute-start.4) | collective-permute-done | bytes 98336 | tf_op jit(solution)/shard_map/ppermute | solution.py:188
  64.1 1.9 %collective-permute-start.8 = (bf16[512,256]{1,0:T(8,128)(2,1)S(1)}, bf16[512,256]{1,0:T(8,128)(2,1)S(1)}, u32[]{:S(2)}, u32[]{:S(2)}) collective-permute-start(bf16[512,256]{1,0:T(8,128)(2,1)S(1)} %pad_maximum_fusion.rest_0_), channel_id=1, source_target_pairs={{0,8},{8,0},{16,24},{24,16},{32,40},{40,32},{48,56},{56,48},{64,72... | collective-permute-start | bytes 786440 | tf_op jit(solution)/shard_map/ppermute | solution.py:169
  66.1 2.4 %collective-permute-start.9 = (bf16[512,256]{1,0:T(8,128)(2,1)S(1)}, bf16[512,256]{1,0:T(8,128)(2,1)S(1)}, u32[]{:S(2)}, u32[]{:S(2)}) collective-permute-start(bf16[512,256]{1,0:T(8,128)(2,1)S(1)} %collective-permute-done.5.rest_1_), channel_id=1, source_target_pairs={{0,8},{8,0},{16,24},{24,16},{32,40},{40,32},{48,56},{56,48},{64,72... | collective-permute-start | bytes 786440 | tf_op jit(solution)/shard_map/ppermute | solution.py:169
  68.5 1.9 %collective-permute-start.10 = (bf16[512,256]{1,0:T(8,128)(2,1)S(1)}, bf16[512,256]{1,0:T(8,128)(2,1)S(1)}, u32[]{:S(2)}, u32[]{:S(2)}) collective-permute-start(bf16[512,256]{1,0:T(8,128)(2,1)S(1)} %collective-permute-done.6.rest_2_), channel_id=1, source_target_pairs={{0,8},{8,0},{16,24},{24,16},{32,40},{40,32},{48,56},{56,48},{64,72... | collective-permute-start | bytes 786440 | tf_op jit(solution)/shard_map/ppermute | solution.py:169
  70.4 2.4 %collective-permute-start.11 = (bf16[512,256]{1,0:T(8,128)(2,1)S(1)}, bf16[512,256]{1,0:T(8,128)(2,1)S(1)}, u32[]{:S(2)}, u32[]{:S(2)}) collective-permute-start(bf16[512,256]{1,0:T(8,128)(2,1)S(1)} %collective-permute-done.7.rest_3_), channel_id=1, source_target_pairs={{0,8},{8,0},{16,24},{24,16},{32,40},{40,32},{48,56},{56,48},{64,72... | collective-permute-start | bytes 786440 | tf_op jit(solution)/shard_map/ppermute | solution.py:169
  72.9 0.1 fusion.3
  73.2 0.8 collective-permute-done.11.rest_7_
  74.0 10.5 %attention.1 = (bf16[128,1024]{1,0:T(8,128)(2,1)S(1)}, bf16[128,1024]{1,0:T(8,128)(2,1)S(1)}) custom-call(s32[768]{0:T(1024)S(1)} %reshape.22.lists_ref, s32[2]{0:T(128)S(1)} %pad_add_fusion.spot_ref, bf16[128,2048]{1,0:T(8,128)(2,1)S(1)} %bitcast.20, bf16[128,1024]{1,0:T(8,128)(2,1)S(1)} %collective-permute-done.3.far_ref, ...), custom_call_target="tpu_custom_call" | custom-call | flops 1879048192 | bytes 4194304 | tf_op jit(solution)/shard_map/attention/pallas_call | solution.py:134
  84.6 45.4 %all_to_all.35 = bf16[8,32,1024]{2,1,0:T(8,128)(2,1)S(1)} all-to-all(bf16[8,32,1024]{2,1,0:T(8,128)(2,1)S(1)} %bitcast.23), channel_id=1, replica_groups=mesh['x'=4,'zc'=16,'y'=4,'zh'=2] {'y','zh'}, dimensions={0} | all-to-all | bytes 1048576 | tf_op jit(solution)/shard_map/all_to_all | solution.py:207
  130.0 0.8 copy.20
  (27 shorter events, 0.4 us)
Async XLA Ops:
  0.0 0.7 copy-start.2
  0.7 11.0 %collective-permute-start = (bf16[64,256]{1,0:T(8,128)(2,1)S(1)}, bf16[64,256]{1,0:T(8,128)(2,1)S(1)}, u32[]{:S(2)}, u32[]{:S(2)}) collective-permute-start(bf16[64,256]{1,0:T(8,128)(2,1)S(1)} %constant_dynamic-update-slice_fusion), channel_id=1, source_target_pairs={{0,64},{8,72},{16,80},{24,88},{32,96},{40,104},{48,112},{56,120},{... | collective-permute-start | bytes 98312 | tf_op jit(solution)/shard_map/ppermute | solution.py:169
  11.7 11.5 %collective-permute-start.1 = (bf16[128,256]{1,0:T(8,128)(2,1)S(1)}, bf16[128,256]{1,0:T(8,128)(2,1)S(1)}, u32[]{:S(2)}, u32[]{:S(2)}) collective-permute-start(bf16[128,256]{1,0:T(8,128)(2,1)S(1)} %pad_maximum_fusion.2), channel_id=1, source_target_pairs={{0,32},{8,40},{16,48},{24,56},{32,0},{40,8},{48,16},{56,24},{64,96... | collective-permute-start | bytes 196616 | tf_op jit(solution)/shard_map/ppermute | solution.py:169
  18.8 13.3 %all-to-all-start = ((bf16[32,4,2048]{2,0,1:T(8,128)(2,1)}), bf16[32,4,2048]{2,0,1:T(8,128)(2,1)S(1)}, u32[]{:S(2)}, u32[]{:S(2)}) async-start(bf16[32,4,2048]{2,0,1:T(8,128)(2,1)} %bitcast.18), calls=%async_computation | async-start | bytes 1048576 | tf_op jit(solution)/shard_map/all_to_all | solution.py:184
  23.3 2.2 %copy-start = (bf16[256,128]{1,0:T(8,128)(2,1)S(1)}, bf16[256,128]{1,0:T(8,128)(2,1)}, u32[]{:S(2)}) copy-start(bf16[256,128]{1,0:T(8,128)(2,1)} %param.9) | copy-start | bytes 196612
  23.3 2.2 %copy-start.1 = (bf16[256,128]{1,0:T(8,128)(2,1)S(1)}, bf16[256,128]{1,0:T(8,128)(2,1)}, u32[]{:S(2)}) copy-start(bf16[256,128]{1,0:T(8,128)(2,1)} %param.10) | copy-start | bytes 196612
  23.3 7.0 %collective-permute-start.2 = (bf16[256,256]{1,0:T(8,128)(2,1)S(1)}, bf16[256,256]{1,0:T(8,128)(2,1)S(1)}, u32[]{:S(2)}, u32[]{:S(2)}) collective-permute-start(bf16[256,256]{1,0:T(8,128)(2,1)S(1)} %pad_maximum_fusion.1), channel_id=1, source_target_pairs={{0,16},{8,24},{16,0},{24,8},{32,48},{40,56},{48,32},{56,40},{64,80... | collective-permute-start | bytes 393224 | tf_op jit(solution)/shard_map/ppermute | solution.py:169
  32.1 34.0 %collective-permute-start.3 = (bf16[128,1024]{1,0:T(8,128)(2,1)S(1)}, bf16[128,1024]{1,0:T(8,128)(2,1)S(1)}, u32[]{:S(2)}, u32[]{:S(2)}) collective-permute-start(bf16[128,1024]{1,0:T(8,128)(2,1)S(1)} %constant_dynamic-slice_fusion), channel_id=1, source_target_pairs={{0,1},{1,0},{2,3},{3,2},{4,5},{5,4},{6,7},{7,6},{8,9},{9,8},{10,11... | collective-permute-start | bytes 786440 | tf_op jit(solution)/shard_map/ppermute | solution.py:172
  43.1 22.9 %collective-permute-start.7 = (bf16[512,256]{1,0:T(8,128)(2,1)S(1)}, bf16[512,256]{1,0:T(8,128)(2,1)S(1)}, u32[]{:S(2)}, u32[]{:S(2)}) collective-permute-start(bf16[512,256]{1,0:T(8,128)(2,1)S(1)} %pad_maximum_fusion.rest_0_), channel_id=1, source_target_pairs={{0,384},{8,392},{16,400},{24,408},{32,416},{40,424},{48,432},{56,4... | collective-permute-start | bytes 786440 | tf_op jit(solution)/shard_map/ppermute | solution.py:169
  45.6 20.5 %collective-permute-start.6 = (bf16[512,256]{1,0:T(8,128)(2,1)S(1)}, bf16[512,256]{1,0:T(8,128)(2,1)S(1)}, u32[]{:S(2)}, u32[]{:S(2)}) collective-permute-start(bf16[512,256]{1,0:T(8,128)(2,1)S(1)} %pad_maximum_fusion.rest_0_), channel_id=1, source_target_pairs={{0,256},{8,264},{16,272},{24,280},{32,288},{40,296},{48,304},{56,3... | collective-permute-start | bytes 786440 | tf_op jit(solution)/shard_map/ppermute | solution.py:169
  49.9 16.2 %collective-permute-start.5 = (bf16[512,256]{1,0:T(8,128)(2,1)S(1)}, bf16[512,256]{1,0:T(8,128)(2,1)S(1)}, u32[]{:S(2)}, u32[]{:S(2)}) collective-permute-start(bf16[512,256]{1,0:T(8,128)(2,1)S(1)} %pad_maximum_fusion.rest_0_), channel_id=1, source_target_pairs={{0,128},{8,136},{16,144},{24,152},{32,160},{40,168},{48,176},{56,1... | collective-permute-start | bytes 786440 | tf_op jit(solution)/shard_map/ppermute | solution.py:169
  53.6 10.5 %collective-permute-start.4 = (bf16[192,256]{1,0:T(8,128)(2,1)S(1)}, bf16[192,256]{1,0:T(8,128)(2,1)S(1)}, u32[]{:S(2)}, u32[]{:S(2)}) collective-permute-start(bf16[192,256]{1,0:T(8,128)(2,1)S(1)} %slice.4), channel_id=1, source_target_pairs={{0,8},{8,16},{16,24},{24,32},{32,40},{40,48},{48,56},{56,64},{64,7... | collective-permute-start | bytes 294920 | tf_op jit(solution)/shard_map/ppermute | solution.py:188
  55.6 17.3 %copy-start.3 = (s32[8,4,24]{2,1,0:T(4,128)S(1)}, s32[8,4,24]{2,1,0:T(4,128)}, u32[]{:S(2)}) copy-start(s32[8,4,24]{2,1,0:T(4,128)} %param.11) | copy-start | bytes 9220
  64.1 9.0 %collective-permute-start.8 = (bf16[512,256]{1,0:T(8,128)(2,1)S(1)}, bf16[512,256]{1,0:T(8,128)(2,1)S(1)}, u32[]{:S(2)}, u32[]{:S(2)}) collective-permute-start(bf16[512,256]{1,0:T(8,128)(2,1)S(1)} %pad_maximum_fusion.rest_0_), channel_id=1, source_target_pairs={{0,8},{8,0},{16,24},{24,16},{32,40},{40,32},{48,56},{56,48},{64,72... | collective-permute-start | bytes 786440 | tf_op jit(solution)/shard_map/ppermute | solution.py:169
  66.1 7.0 %collective-permute-start.9 = (bf16[512,256]{1,0:T(8,128)(2,1)S(1)}, bf16[512,256]{1,0:T(8,128)(2,1)S(1)}, u32[]{:S(2)}, u32[]{:S(2)}) collective-permute-start(bf16[512,256]{1,0:T(8,128)(2,1)S(1)} %collective-permute-done.5.rest_1_), channel_id=1, source_target_pairs={{0,8},{8,0},{16,24},{24,16},{32,40},{40,32},{48,56},{56,48},{64,72... | collective-permute-start | bytes 786440 | tf_op jit(solution)/shard_map/ppermute | solution.py:169
  68.5 4.6 %collective-permute-start.10 = (bf16[512,256]{1,0:T(8,128)(2,1)S(1)}, bf16[512,256]{1,0:T(8,128)(2,1)S(1)}, u32[]{:S(2)}, u32[]{:S(2)}) collective-permute-start(bf16[512,256]{1,0:T(8,128)(2,1)S(1)} %collective-permute-done.6.rest_2_), channel_id=1, source_target_pairs={{0,8},{8,0},{16,24},{24,16},{32,40},{40,32},{48,56},{56,48},{64,72... | collective-permute-start | bytes 786440 | tf_op jit(solution)/shard_map/ppermute | solution.py:169
  70.4 3.6 %collective-permute-start.11 = (bf16[512,256]{1,0:T(8,128)(2,1)S(1)}, bf16[512,256]{1,0:T(8,128)(2,1)S(1)}, u32[]{:S(2)}, u32[]{:S(2)}) collective-permute-start(bf16[512,256]{1,0:T(8,128)(2,1)S(1)} %collective-permute-done.7.rest_3_), channel_id=1, source_target_pairs={{0,8},{8,0},{16,24},{24,16},{32,40},{40,32},{48,56},{56,48},{64,72... | collective-permute-start | bytes 786440 | tf_op jit(solution)/shard_map/ppermute | solution.py:169

commit v4 on v2

--- a/solution.py
+++ b/solution.py
@@ -14,7 +14,7 @@
 WIN = 4
 X, ZL, CORE = 4, 8, 2
 NEG = -1e30
-HEADS_A_STEP = 4
+HEADS_A_STEP = 8
 
 
 def attention_kernel(

time: 127 us -> 127 us (level)
  no operation moved by 1% of the time
where the time goes in v4:
time: 127 us; the launch traced here: 126 us
  starting transfers between devices  55.8 us (44%)
  blocking collectives  41.7 us (33%)
  waiting for transfers between devices  13 us (10%)
  Pallas kernels  9.98 us (8%)
  local copies, waits for them, and re-layouts  5.36 us (4%)
    all_to_all x1, blocking collectives, per_device(): lax.all_to_all(both, ('y', 'zh'), split_axis=0, concat_axis=1, tiled=True)  41.7 us
    ppermute x4, starting transfers between devices, send(): lax.ppermute(array, ('x', 'zc'), [(i, target(i)) for i in range(count)])  27.1 us
    ppermute x1, starting transfers between devices, over_side(): return lax.ppermute(array, 'zh', [(0, 1), (1, 0)])  12.8 us
    pallas_call x1, Pallas kernels, attention(): pl.pallas_call(functools.partial(attention_kernel, pieces=len(pieces), bl...  9.98 us
    ppermute x1, waiting for transfers between devices, per_device(): lax.ppermute(tail, ('x', 'zc'), [(i, i + 1) for i in range(count - 1)])  7.41 us
    ppermute x1, starting transfers between devices, per_device(): lax.ppermute(tail, ('x', 'zc'), [(i, i + 1) for i in range(count - 1)])  7.38 us
    ppermute x4, waiting for transfers between devices, send(): lax.ppermute(array, ('x', 'zc'), [(i, target(i)) for i in range(count)])  5.12 us
    all_to_all x1, starting transfers between devices, per_device(): lax.all_to_all(copies, 'x', split_axis=0, concat_axis=0, tiled=True)  4.26 us
  transfers between devices with their start and end apart: 8, of which 5 were waited for; matrix products, arithmetic and copies ran while one was open for 2% of the time, Pallas kernels for 0%

profile of v4, /device:TPU:67, one launch (start us, length us, event | category | flops | bytes accessed | tf_op | source)
XLA Modules:
  0.0 126.3 jit_solution(16900585622772859753)
XLA Ops:
  0.0 0.7 constant_dynamic-update-slice_fusion.1
  0.7 8.8 %collective-permute-start = (bf16[64,256]{1,0:T(8,128)(2,1)S(1)}, bf16[64,256]{1,0:T(8,128)(2,1)S(1)}, u32[]{:S(2)}, u32[]{:S(2)}) collective-permute-start(bf16[64,256]{1,0:T(8,128)(2,1)S(1)} %constant_dynamic-update-slice_fusion), channel_id=1, source_target_pairs={{0,64},{8,72},{16,80},{24,88},{32,96},{40,104},{48,112},{56,120},{... | collective-permute-start | bytes 98312 | tf_op jit(solution)/shard_map/ppermute | solution.py:169
  9.6 1.3 %collective-permute-done = bf16[64,256]{1,0:T(8,128)(2,1)S(1)} collective-permute-done((bf16[64,256]{1,0:T(8,128)(2,1)S(1)}, bf16[64,256]{1,0:T(8,128)(2,1)S(1)}, u32[]{:S(2)}, u32[]{:S(2)}) %collective-permute-start) | collective-permute-done | bytes 32800 | tf_op jit(solution)/shard_map/ppermute | solution.py:169
  10.9 1.9 %collective-permute-start.1 = (bf16[128,256]{1,0:T(8,128)(2,1)S(1)}, bf16[128,256]{1,0:T(8,128)(2,1)S(1)}, u32[]{:S(2)}, u32[]{:S(2)}) collective-permute-start(bf16[128,256]{1,0:T(8,128)(2,1)S(1)} %pad_maximum_fusion.2), channel_id=1, source_target_pairs={{0,32},{8,40},{16,48},{24,56},{32,0},{40,8},{48,16},{56,24},{64,96... | collective-permute-start | bytes 196616 | tf_op jit(solution)/shard_map/ppermute | solution.py:169
  12.8 1.9 %copy.22 = bf16[4,4,8,2048]{3,2,0,1:T(8,128)(2,1)} copy(bf16[4,4,8,2048]{3,2,1,0:T(8,128)(2,1)} %bitcast.28) | data formatting | bytes 1048576 | tf_op jit(solution)/shard_map/all_to_all | solution.py:184
  14.7 4.2 %all-to-all-start = ((bf16[32,4,2048]{2,0,1:T(8,128)(2,1)}), bf16[32,4,2048]{2,0,1:T(8,128)(2,1)S(1)}, u32[]{:S(2)}, u32[]{:S(2)}) async-start(bf16[32,4,2048]{2,0,1:T(8,128)(2,1)} %bitcast.19), calls=%async_computation | async-start | bytes 1048576 | tf_op jit(solution)/shard_map/all_to_all | solution.py:184
  18.9 4.2 %collective-permute-start.2 = (bf16[256,256]{1,0:T(8,128)(2,1)S(1)}, bf16[256,256]{1,0:T(8,128)(2,1)S(1)}, u32[]{:S(2)}, u32[]{:S(2)}) collective-permute-start(bf16[256,256]{1,0:T(8,128)(2,1)S(1)} %pad_maximum_fusion.1), channel_id=1, source_target_pairs={{0,16},{8,24},{16,0},{24,8},{32,48},{40,56},{48,32},{56,40},{64,80... | collective-permute-start | bytes 393224 | tf_op jit(solution)/shard_map/ppermute | solution.py:169
  23.2 2.5 %collective-permute-done.2 = bf16[256,256]{1,0:T(8,128)(2,1)S(1)} collective-permute-done((bf16[256,256]{1,0:T(8,128)(2,1)S(1)}, bf16[256,256]{1,0:T(8,128)(2,1)S(1)}, u32[]{:S(2)}, u32[]{:S(2)}) %collective-permute-start.2) | collective-permute-done | bytes 131104 | tf_op jit(solution)/shard_map/ppermute | solution.py:169
  25.7 0.5 all-to-all-done
  26.3 1.1 broadcast_in_dim.14
  27.3 4.3 %all-to-all-start.1 = ((bf16[4,512,256]{2,1,0:T(8,128)(2,1)}), bf16[4,512,256]{2,1,0:T(8,128)(2,1)S(1)}, u32[]{:S(2)}, u32[]{:S(2)}) async-start(bf16[4,512,256]{2,1,0:T(8,128)(2,1)} %broadcast_in_dim.14), calls=%async_computation.1 | async-start | bytes 2097152 | tf_op jit(solution)/shard_map/all_to_all | solution.py:190
  31.6 12.8 %collective-permute-start.3 = (bf16[128,1024]{1,0:T(8,128)(2,1)S(1)}, bf16[128,1024]{1,0:T(8,128)(2,1)S(1)}, u32[]{:S(2)}, u32[]{:S(2)}) collective-permute-start(bf16[128,1024]{1,0:T(8,128)(2,1)S(1)} %constant_dynamic-slice_fusion), channel_id=1, source_target_pairs={{0,1},{1,0},{2,3},{3,2},{4,5},{5,4},{6,7},{7,6},{8,9},{9,8},{10,11... | collective-permute-start | bytes 786440 | tf_op jit(solution)/shard_map/ppermute | solution.py:172
  44.4 7.4 %collective-permute-start.4 = (bf16[192,256]{1,0:T(8,128)(2,1)S(1)}, bf16[192,256]{1,0:T(8,128)(2,1)S(1)}, u32[]{:S(2)}, u32[]{:S(2)}) collective-permute-start(bf16[192,256]{1,0:T(8,128)(2,1)S(1)} %slice.4), channel_id=1, source_target_pairs={{0,8},{8,16},{16,24},{24,32},{32,40},{40,48},{48,56},{56,64},{64,7... | collective-permute-start | bytes 294920 | tf_op jit(solution)/shard_map/ppermute | solution.py:187
  51.8 7.4 %collective-permute-done.4.halo_ref = bf16[192,256]{1,0:T(8,128)(2,1)S(1)} collective-permute-done((bf16[192,256]{1,0:T(8,128)(2,1)S(1)}, bf16[192,256]{1,0:T(8,128)(2,1)S(1)}, u32[]{:S(2)}, u32[]{:S(2)}) %collective-permute-start.4) | collective-permute-done | bytes 98336 | tf_op jit(solution)/shard_map/ppermute | solution.py:187
  59.2 12.2 %collective-permute-start.5 = (bf16[2048,256]{1,0:T(8,128)(2,1)S(1)}, bf16[2048,256]{1,0:T(8,128)(2,1)S(1)}, u32[]{:S(2)}, u32[]{:S(2)}) collective-permute-start(bf16[2048,256]{1,0:T(8,128)(2,1)S(1)} %bitcast.22), channel_id=1, source_target_pairs={{0,8},{8,0},{16,24},{24,16},{32,40},{40,32},{48,56},{56,48},{64,72... | collective-permute-start | bytes 3145736 | tf_op jit(solution)/shard_map/ppermute | solution.py:169
  71.5 0.7 copy-done.3
  72.2 0.1 fusion.3
  72.2 0.1 reshape.26.lists_ref
  72.3 0.1 pad_add_fusion.spot_ref
  72.4 1.3 %collective-permute-done.5.rest_1_ = bf16[2048,256]{1,0:T(8,128)(2,1)S(1)} collective-permute-done((bf16[2048,256]{1,0:T(8,128)(2,1)S(1)}, bf16[2048,256]{1,0:T(8,128)(2,1)S(1)}, u32[]{:S(2)}, u32[]{:S(2)}) %collective-permute-start.5) | collective-permute-done | bytes 1048608 | tf_op jit(solution)/shard_map/ppermute | solution.py:169
  73.7 10.0 %attention.1 = (bf16[128,1024]{1,0:T(8,128)(2,1)S(1)}, bf16[128,1024]{1,0:T(8,128)(2,1)S(1)}) custom-call(s32[768]{0:T(1024)S(1)} %reshape.26.lists_ref, s32[2]{0:T(128)S(1)} %pad_add_fusion.spot_ref, bf16[128,2048]{1,0:T(8,128)(2,1)S(1)} %bitcast.21, bf16[128,1024]{1,0:T(8,128)(2,1)S(1)} %collective-permute-done.3.far_ref, ...), custom_call_target="tpu_custom_call" | custom-call | flops 1879048192 | bytes 4194304 | tf_op jit(solution)/shard_map/attention/pallas_call | solution.py:134
  83.7 0.1 maximum_select_fusion
  83.7 41.7 %all_to_all.40 = bf16[8,32,1024]{2,1,0:T(8,128)(2,1)S(1)} all-to-all(bf16[8,32,1024]{2,1,0:T(8,128)(2,1)S(1)} %bitcast.26), channel_id=1, replica_groups=mesh['x'=4,'zc'=16,'y'=4,'zh'=2] {'y','zh'}, dimensions={0} | all-to-all | bytes 1048576 | tf_op jit(solution)/shard_map/all_to_all | solution.py:208
  125.5 0.8 copy.20
  (18 shorter events, 0.1 us)
Async XLA Ops:
  0.0 0.7 copy-start.2
  0.7 10.1 %collective-permute-start = (bf16[64,256]{1,0:T(8,128)(2,1)S(1)}, bf16[64,256]{1,0:T(8,128)(2,1)S(1)}, u32[]{:S(2)}, u32[]{:S(2)}) collective-permute-start(bf16[64,256]{1,0:T(8,128)(2,1)S(1)} %constant_dynamic-update-slice_fusion), channel_id=1, source_target_pairs={{0,64},{8,72},{16,80},{24,88},{32,96},{40,104},{48,112},{56,120},{... | collective-permute-start | bytes 98312 | tf_op jit(solution)/shard_map/ppermute | solution.py:169
  10.9 8.0 %collective-permute-start.1 = (bf16[128,256]{1,0:T(8,128)(2,1)S(1)}, bf16[128,256]{1,0:T(8,128)(2,1)S(1)}, u32[]{:S(2)}, u32[]{:S(2)}) collective-permute-start(bf16[128,256]{1,0:T(8,128)(2,1)S(1)} %pad_maximum_fusion.2), channel_id=1, source_target_pairs={{0,32},{8,40},{16,48},{24,56},{32,0},{40,8},{48,16},{56,24},{64,96... | collective-permute-start | bytes 196616 | tf_op jit(solution)/shard_map/ppermute | solution.py:169
  14.7 11.6 %all-to-all-start = ((bf16[32,4,2048]{2,0,1:T(8,128)(2,1)}), bf16[32,4,2048]{2,0,1:T(8,128)(2,1)S(1)}, u32[]{:S(2)}, u32[]{:S(2)}) async-start(bf16[32,4,2048]{2,0,1:T(8,128)(2,1)} %bitcast.19), calls=%async_computation | async-start | bytes 1048576 | tf_op jit(solution)/shard_map/all_to_all | solution.py:184
  18.9 4.2 %copy-start = (bf16[256,128]{1,0:T(8,128)(2,1)S(1)}, bf16[256,128]{1,0:T(8,128)(2,1)}, u32[]{:S(2)}) copy-start(bf16[256,128]{1,0:T(8,128)(2,1)} %param.9) | copy-start | bytes 196612
  18.9 4.2 %copy-start.1 = (bf16[256,128]{1,0:T(8,128)(2,1)S(1)}, bf16[256,128]{1,0:T(8,128)(2,1)}, u32[]{:S(2)}) copy-start(bf16[256,128]{1,0:T(8,128)(2,1)} %param.10) | copy-start | bytes 196612
  18.9 6.8 %collective-permute-start.2 = (bf16[256,256]{1,0:T(8,128)(2,1)S(1)}, bf16[256,256]{1,0:T(8,128)(2,1)S(1)}, u32[]{:S(2)}, u32[]{:S(2)}) collective-permute-start(bf16[256,256]{1,0:T(8,128)(2,1)S(1)} %pad_maximum_fusion.1), channel_id=1, source_target_pairs={{0,16},{8,24},{16,0},{24,8},{32,48},{40,56},{48,32},{56,40},{64,80... | collective-permute-start | bytes 393224 | tf_op jit(solution)/shard_map/ppermute | solution.py:169
  27.3 31.9 %all-to-all-start.1 = ((bf16[4,512,256]{2,1,0:T(8,128)(2,1)}), bf16[4,512,256]{2,1,0:T(8,128)(2,1)S(1)}, u32[]{:S(2)}, u32[]{:S(2)}) async-start(bf16[4,512,256]{2,1,0:T(8,128)(2,1)} %broadcast_in_dim.14), calls=%async_computation.1 | async-start | bytes 2097152 | tf_op jit(solution)/shard_map/all_to_all | solution.py:190
  31.6 27.6 %collective-permute-start.3 = (bf16[128,1024]{1,0:T(8,128)(2,1)S(1)}, bf16[128,1024]{1,0:T(8,128)(2,1)S(1)}, u32[]{:S(2)}, u32[]{:S(2)}) collective-permute-start(bf16[128,1024]{1,0:T(8,128)(2,1)S(1)} %constant_dynamic-slice_fusion), channel_id=1, source_target_pairs={{0,1},{1,0},{2,3},{3,2},{4,5},{5,4},{6,7},{7,6},{8,9},{9,8},{10,11... | collective-permute-start | bytes 786440 | tf_op jit(solution)/shard_map/ppermute | solution.py:172
  44.4 14.8 %collective-permute-start.4 = (bf16[192,256]{1,0:T(8,128)(2,1)S(1)}, bf16[192,256]{1,0:T(8,128)(2,1)S(1)}, u32[]{:S(2)}, u32[]{:S(2)}) collective-permute-start(bf16[192,256]{1,0:T(8,128)(2,1)S(1)} %slice.4), channel_id=1, source_target_pairs={{0,8},{8,16},{16,24},{24,32},{32,40},{40,48},{48,56},{56,64},{64,7... | collective-permute-start | bytes 294920 | tf_op jit(solution)/shard_map/ppermute | solution.py:187
  59.2 14.5 %collective-permute-start.5 = (bf16[2048,256]{1,0:T(8,128)(2,1)S(1)}, bf16[2048,256]{1,0:T(8,128)(2,1)S(1)}, u32[]{:S(2)}, u32[]{:S(2)}) collective-permute-start(bf16[2048,256]{1,0:T(8,128)(2,1)S(1)} %bitcast.22), channel_id=1, source_target_pairs={{0,8},{8,0},{16,24},{24,16},{32,40},{40,32},{48,56},{56,48},{64,72... | collective-permute-start | bytes 3145736 | tf_op jit(solution)/shard_map/ppermute | solution.py:169
  71.4 0.7 copy-start.3
